TPU v7x, 512 devices: a whole 4x4x16 slice. The times are simulated.
512 devices in a mesh: tm: 16 (over x, y), tile: 32 (over z, core).
Axes of the slice: x: 4, y: 4, z: 16, core: 2. Of those that a mesh axis runs over, the one named last changes fastest.
Arguments:
- haar_video: bfloat16 [64, 128, 6144], P('tm', 'tile'), may hold values from -6 to 6
- clip_lengths: int32 [16], replicated, may hold values from 1 to 8, 64 in all
- block_owner: int32 [16], replicated, may hold values from 0 to 15, each once
- spatial_in: bfloat16 [3, 3, 48, 128], replicated, may hold values from -0.3125 to 0.3125
- temporal_in: bfloat16 [3, 128, 128], replicated, may hold values from -0.3125 to 0.3125
- bias_in: float32 [128], replicated, may hold values from -4 to 4
- spatial_down: bfloat16 [3, 3, 128, 256], replicated, may hold values from -0.25 to 0.25
- temporal_down: bfloat16 [3, 256, 256], replicated, may hold values from -0.25 to 0.25
- bias_down: float32 [256], replicated, may hold values from -4 to 4
- spatial_out: bfloat16 [3, 3, 256, 256], replicated, may hold values from -0.1875 to 0.1875
- temporal_out: bfloat16 [3, 256, 256], replicated, may hold values from -0.25 to 0.25
- bias_out: float32 [256], replicated, may hold values from -3 to 3
Outputs:
- latents: bfloat16 [32, 64, 64, 256], P('tm', 'tile')
Inputs may be any that keep to these rules, and one draw needn't show every extreme that they name: `clip_lengths`: the clip lengths sum to 64; the longest is exactly 8. `block_owner`: every tm index is named exactly once.
All inputs are finite; a program needn't handle non-finite values.
Results may differ from a plain program's by a relative error of at most 0.015.
Values may be sent and summed in bfloat16 or wider, within the bound.
A program may use at most 64 MiB of HBM per device.

v0:
```python
from functools import partial

import jax
import jax.numpy as jnp
from jax import lax
from jax.sharding import PartitionSpec as P


def padded_2(block, sides, width):
    for axis, dim in sides:
        count = lax.axis_size(axis)
        forward = [(i, i + 1) for i in range(count - 1)]
        backward = [(target, source) for source, target in forward]
        low = lax.ppermute(
            lax.slice_in_dim(block, block.shape[dim] - width, None, axis=dim), axis, forward
        )
        high = lax.ppermute(lax.slice_in_dim(block, 0, width, axis=dim), axis, backward)
        block = jnp.concatenate([low, block, high], axis=dim)
    return block


def passed_along(block, axis, distance):
    devices = range(lax.axis_size(axis))
    route = [(i - distance, i) for i in devices if i - distance in devices]
    return lax.ppermute(block, axis, route)


def clip_of(frame_ids, clip_lengths):
    clip_ends = jnp.cumsum(clip_lengths)
    return jnp.sum((clip_ends[None, :] <= frame_ids[:, None]).astype(jnp.int32), axis=1)


def tap_mask(key_frames, tap_frames, clip_lengths):
    tap_clips = clip_of(tap_frames.reshape(-1), clip_lengths).reshape(tap_frames.shape)
    same_clip = tap_clips == clip_of(key_frames, clip_lengths)[:, None]
    return jnp.where(same_clip & (tap_frames >= 0), 1.0, 0.0).astype(jnp.bfloat16)


def spatial_conv(row_extended, kernel, stride, out_rows, out_cols):
    pad_right = 1 if stride == 1 else 0
    padded = jnp.pad(row_extended, ((0, 0), (0, 0), (1, pad_right), (0, 0)))
    pieces = [
        padded[
            :,
            row_tap : row_tap + stride * out_rows : stride,
            col_tap : col_tap + stride * out_cols : stride,
        ]
        for row_tap in range(3)
        for col_tap in range(3)
    ]
    patches = jnp.concatenate(pieces, axis=-1)
    flattened = jnp.dot(
        patches.reshape(-1, patches.shape[-1]),
        kernel.reshape(-1, kernel.shape[-1]),
        preferred_element_type=jnp.float32,
    )
    return flattened.reshape(patches.shape[:-1] + (kernel.shape[-1],))


def temporal_conv(extended, kernel, mask, out_count, stride, bias, activate):
    running = None
    for lag in range(3):
        tap_frames = extended[lag : lag + stride * out_count : stride] * mask[:, lag].reshape(
            (-1, 1, 1, 1)
        )
        tap_term = jnp.dot(
            tap_frames.reshape(-1, tap_frames.shape[-1]),
            kernel[lag],
            preferred_element_type=jnp.float32,
        )
        running = tap_term if running is None else running + tap_term
    running = running + bias
    if activate:
        running = jax.nn.silu(running)
    return running.reshape(tap_frames.shape[:-1] + (kernel.shape[-1],)).astype(jnp.bfloat16)


def pick_rows(running, shard_piece, first_row, owners, my_index, block_span):
    row_total = shard_piece.shape[0]
    row_ids = jnp.arange(row_total, dtype=jnp.int32)
    block_ids = row_ids // block_span
    slot_ids = jnp.arange(owners.shape[0], dtype=jnp.int32)
    owner_of = jnp.sum(
        jnp.where(block_ids[:, None] == slot_ids[None, :], owners[None, :], 0), axis=1
    )
    position = row_ids % block_span
    span_ids = jnp.arange(block_span, dtype=jnp.int32)
    select = ((position[None, :] == span_ids[:, None]) & (owner_of[None, :] == my_index)).astype(
        jnp.bfloat16
    )
    return jnp.dot(select, shard_piece, preferred_element_type=jnp.float32)


def third_mask(block_index, reduced_count, clip_lengths):
    reduced_ids = block_index * reduced_count + jnp.arange(reduced_count, dtype=jnp.int32)
    lags = jnp.arange(3, dtype=jnp.int32)
    reduced_taps = reduced_ids[:, None] + lags[None, :] - 2
    return tap_mask(2 * reduced_ids + 1, 2 * reduced_taps + 1, clip_lengths)


def per_device(
    haar_video,
    clip_lengths,
    block_owner,
    spatial_in,
    temporal_in,
    bias_in,
    spatial_down,
    temporal_down,
    bias_down,
    spatial_out,
    temporal_out,
    bias_out,
):
    frame_count, row_count, flat_width = haar_video.shape
    in_channels = spatial_in.shape[2]
    col_count = flat_width // in_channels
    frames = haar_video.reshape(frame_count, row_count, col_count, in_channels)
    my_index = lax.axis_index("tm")
    lags = jnp.arange(3, dtype=jnp.int32)
    row_extended = padded_2(frames, (("tile", 1),), 1)
    spatial_one = spatial_conv(row_extended, spatial_in, 1, row_count, col_count).astype(
        jnp.bfloat16
    )
    context = passed_along(spatial_one[frame_count - 2 :], "tm", 1)
    extended = jnp.concatenate([context, spatial_one], axis=0)
    frame_ids = my_index * frame_count + jnp.arange(frame_count, dtype=jnp.int32)
    causal_mask = tap_mask(frame_ids, frame_ids[:, None] + lags[None, :] - 2, clip_lengths)
    hidden_one = temporal_conv(extended, temporal_in, causal_mask, frame_count, 1, bias_in, True)
    upper_row = passed_along(hidden_one[:, row_count - 1 :], "tile", 1)
    row_extended = jnp.concatenate([upper_row, hidden_one], axis=1)
    reduced_rows = row_count // 2
    reduced_cols = col_count // 2
    reduced_count = frame_count // 2
    spatial_two = spatial_conv(row_extended, spatial_down, 2, reduced_rows, reduced_cols).astype(
        jnp.bfloat16
    )
    prior_frame = passed_along(spatial_two[frame_count - 1 :], "tm", 1)
    extended = jnp.concatenate([prior_frame, spatial_two], axis=0)
    reduced_ids = my_index * reduced_count + jnp.arange(reduced_count, dtype=jnp.int32)
    strided_mask = tap_mask(
        2 * reduced_ids + 1, 2 * reduced_ids[:, None] + lags[None, :] - 1, clip_lengths
    )
    hidden_two = temporal_conv(
        extended, temporal_down, strided_mask, reduced_count, 2, bias_down, True
    )
    context = passed_along(hidden_two, "tm", 1)
    extended = jnp.concatenate([context, hidden_two], axis=0)
    block_span = extended.shape[0]
    flattened = extended.reshape(block_span, -1)
    gather_fn = partial(pick_rows, owners=block_owner, my_index=my_index, block_span=block_span)
    moved_block = gather_fn(
        jnp.zeros(flattened.shape, jnp.float32),
        lax.all_gather(flattened, "tm", axis=0, tiled=True),
        jnp.int32(0),
    )
    moved_block = moved_block.astype(jnp.bfloat16).reshape(extended.shape)
    slot_ids = jnp.arange(block_owner.shape[0], dtype=jnp.int32)
    source_block = jnp.sum(jnp.where(block_owner == my_index, slot_ids, 0))
    row_extended = padded_2(moved_block, (("tile", 1),), 1)
    spatial_three = spatial_conv(row_extended, spatial_out, 1, reduced_rows, reduced_cols).astype(
        jnp.bfloat16
    )
    last_mask = third_mask(source_block, reduced_count, clip_lengths)
    final_block = temporal_conv(
        spatial_three, temporal_out, last_mask, reduced_count, 1, bias_out, False
    )
    return final_block


def solution(mesh):
    placed = (P("tm", "tile", None), P(), P(), P(), P(), P(), P(), P(), P(), P(), P(), P())
    return jax.shard_map(
        per_device,
        mesh=mesh,
        in_specs=placed,
        out_specs=P("tm", "tile", None, None),
        check_vma=False,
    )
```

profile of v0, /device:TPU:1, one launch (start us, length us, event | category | flops | bytes accessed | tf_op | source)
XLA Modules:
  0.0 164.1 jit_solution(17710069117527432567)
XLA Ops:
  6.5 1.5 reshape.216
  8.1 0.2 copy.28
  8.3 4.9 %collective-permute-start = (bf16[4,1,128,48]{2,3,1,0:T(8,128)(2,1)S(1)}, bf16[4,1,128,48]{2,3,1,0:T(8,128)(2,1)S(1)}, u32[]{:S(2)}, u32[]{:S(2)}) collective-permute-start(bf16[4,1,128,48]{2,3,1,0:T(8,128)(2,1)S(1)} %get-tuple-element.28), channel_id=1, source_target_pairs={{0,1},{1,2},{2,3},{3,4},{4,5},{5,6},{6,7},{7,8},{8,9},{9,10},{10,1... | collective-permute-start | bytes 147464 | tf_op jit(solution)/shard_map/ppermute | solution.py:14
  13.3 5.1 %collective-permute-start.1 = (bf16[4,1,128,48]{2,3,1,0:T(8,128)(2,1)S(1)}, bf16[4,1,128,48]{2,3,1,0:T(8,128)(2,1)S(1)}, u32[]{:S(2)}, u32[]{:S(2)}) collective-permute-start(bf16[4,1,128,48]{2,3,1,0:T(8,128)(2,1)S(1)} %get-tuple-element.29), channel_id=1, source_target_pairs={{1,0},{2,1},{3,2},{4,3},{5,4},{6,5},{7,6},{8,7},{9,8},{10,9},{11,1... | collective-permute-start | bytes 147464 | tf_op jit(solution)/shard_map/ppermute | solution.py:17
  18.6 0.7 copy.34
  19.9 1.3 fusion.55
  22.3 0.3 fusion.16
  23.5 0.8 convolution_convert_fusion.1
  24.3 1.3 collective-permute-start.2
  25.6 0.2 convert_reduce_fusion.1
  25.9 0.2 slice_reduce_fusion
  26.1 0.2 fusion.50
  26.4 4.9 %collective-permute-done.2 = bf16[2,4,128,128]{3,2,1,0:T(8,128)(2,1)S(1)} collective-permute-done((bf16[2,4,128,128]{3,2,1,0:T(8,128)(2,1)S(1)}, bf16[2,4,128,128]{3,2,1,0:T(8,128)(2,1)S(1)}, u32[]{:S(2)}, u32[]{:S(2)}) %collective-permute-start.2) | collective-permute-done | bytes 262176 | tf_op jit(solution)/shard_map/ppermute | solution.py:25
  31.5 0.3 fusion.42
  31.8 0.3 convolution_add_fusion.1
  32.1 0.4 multiply_convert_fusion
  32.6 3.0 %collective-permute-start.3 = (bf16[4,1,128,128]{3,2,1,0:T(8,128)(2,1)S(1)}, bf16[4,1,128,128]{3,2,1,0:T(8,128)(2,1)S(1)}, u32[]{:S(2)}, u32[]{:S(2)}) collective-permute-start(bf16[4,1,128,128]{3,2,1,0:T(8,128)(2,1)S(1)} %slice.255), channel_id=1, source_target_pairs={{0,1},{1,2},{2,3},{3,4},{4,5},{5,6},{6,7},{7,8},{8,9},{9,10},{10,1... | collective-permute-start | bytes 393224 | tf_op jit(solution)/shard_map/ppermute | solution.py:25
  35.6 0.2 slice_reduce_fusion.6
  35.9 1.6 collective-permute-done.3
  37.7 0.3 slice.206
  38.0 0.3 slice.207
  38.3 0.3 slice.208
  38.6 0.3 slice.209
  39.0 0.3 slice.210
  39.3 0.3 slice.211
  39.6 0.4 slice.212
  40.1 0.4 slice.213
  40.5 0.8 slice.214
  41.8 0.7 copy-done.6
  42.5 0.5 convolution_convert_fusion.3
  43.0 4.1 %collective-permute-start.4 = (bf16[1,2,64,256]{3,2,1,0:T(8,128)(2,1)S(1)}, bf16[1,2,64,256]{3,2,1,0:T(8,128)(2,1)S(1)}, u32[]{:S(2)}, u32[]{:S(2)}) collective-permute-start(bf16[1,2,64,256]{3,2,1,0:T(8,128)(2,1)S(1)} %slice.256), channel_id=1, source_target_pairs={{0,32},{32,64},{64,96},{96,128},{128,160},{160,192},{192,224},{224... | collective-permute-start | bytes 196616 | tf_op jit(solution)/shard_map/ppermute | solution.py:25
  47.2 1.2 collective-permute-done.4
  48.8 0.2 convolution_add_fusion.5
  49.0 0.2 multiply_convert_fusion.1
  49.2 3.7 %collective-permute-start.5 = (bf16[2,2,64,256]{3,2,1,0:T(8,128)(2,1)S(1)}, bf16[2,2,64,256]{3,2,1,0:T(8,128)(2,1)S(1)}, u32[]{:S(2)}, u32[]{:S(2)}) collective-permute-start(bf16[2,2,64,256]{3,2,1,0:T(8,128)(2,1)S(1)} %bitcast.94), channel_id=1, source_target_pairs={{0,32},{32,64},{64,96},{96,128},{128,160},{160,192},{192,224},{224... | collective-permute-start | bytes 393224 | tf_op jit(solution)/shard_map/ppermute | solution.py:25
  52.9 3.2 %collective-permute-done.5 = bf16[2,2,64,256]{3,2,1,0:T(8,128)(2,1)S(1)} collective-permute-done((bf16[2,2,64,256]{3,2,1,0:T(8,128)(2,1)S(1)}, bf16[2,2,64,256]{3,2,1,0:T(8,128)(2,1)S(1)}, u32[]{:S(2)}, u32[]{:S(2)}) %collective-permute-start.5) | collective-permute-done | bytes 131104 | tf_op jit(solution)/shard_map/ppermute | solution.py:25
  56.1 0.9 reshape.236
  57.2 77.2 %all-gather.3.cloned.1.call-done = bf16[16,4,32768]{2,1,0:T(4,128)(2,1)} async-done(((bf16[1,4,32768]{2,1,0:T(4,128)(2,1)}), bf16[16,4,32768]{2,1,0:T(4,128)(2,1)}) %all-gather.3.cloned.1.call-update) | async-done | bytes 4194320 | tf_op jit(solution)/shard_map/all_gather | solution.py:154
  134.4 7.0 %reshape.237 = bf16[64,32768]{1,0:T(8,128)(2,1)} reshape(bf16[16,4,32768]{2,1,0:T(4,128)(2,1)} %all-gather.3.cloned.1.call-done) | data formatting | bytes 8388608
  141.3 2.8 %convolution_convert_fusion = bf16[4,32768]{1,0:T(4,128)(2,1)S(1)} fusion(bf16[64,32768]{1,0:T(8,128)(2,1)} %reshape.237, s32[64]{0:T(128)S(1)} %and_select_fusion.3, pred[64]{0:T(512)(128)(4,1)S(1)} %broadcast_compare_fusion), kind=kOutput, calls=%fused_computation | convolution fusion | flops 16908800 | bytes 4456768 | tf_op jit(solution)/shard_map/dot_general | solution.py:91
  144.2 3.7 %collective-permute-start.6 = (bf16[4,1,64,256]{3,2,1,0:T(8,128)(2,1)S(1)}, bf16[4,1,64,256]{3,2,1,0:T(8,128)(2,1)S(1)}, u32[]{:S(2)}, u32[]{:S(2)}) collective-permute-start(bf16[4,1,64,256]{3,2,1,0:T(8,128)(2,1)S(1)} %get-tuple-element.24), channel_id=1, source_target_pairs={{0,1},{1,2},{2,3},{3,4},{4,5},{5,6},{6,7},{7,8},{8,9},{9,10},{10,1... | collective-permute-start | bytes 393224 | tf_op jit(solution)/shard_map/ppermute | solution.py:14
  148.0 1.9 %collective-permute-start.7 = (bf16[4,1,64,256]{3,2,1,0:T(8,128)(2,1)S(1)}, bf16[4,1,64,256]{3,2,1,0:T(8,128)(2,1)S(1)}, u32[]{:S(2)}, u32[]{:S(2)}) collective-permute-start(bf16[4,1,64,256]{3,2,1,0:T(8,128)(2,1)S(1)} %get-tuple-element.25), channel_id=1, source_target_pairs={{1,0},{2,1},{3,2},{4,3},{5,4},{6,5},{7,6},{8,7},{9,8},{10,9},{11,1... | collective-permute-start | bytes 393224 | tf_op jit(solution)/shard_map/ppermute | solution.py:17
  150.0 0.2 slice_reduce_fusion.3
  150.2 4.1 %collective-permute-done.7 = bf16[4,1,64,256]{3,2,1,0:T(8,128)(2,1)S(1)} collective-permute-done((bf16[4,1,64,256]{3,2,1,0:T(8,128)(2,1)S(1)}, bf16[4,1,64,256]{3,2,1,0:T(8,128)(2,1)S(1)}, u32[]{:S(2)}, u32[]{:S(2)}) %collective-permute-start.7) | collective-permute-done | bytes 131104 | tf_op jit(solution)/shard_map/ppermute | solution.py:17
  154.3 0.2 fusion.18
  154.9 0.8 convolution_convert_fusion.2
  156.1 0.2 convolution_add_fusion.3
  156.4 0.8 fusion.7
  (89 shorter events, 4.5 us)
Async XLA Ops:
  6.5 148.3 %copy-start = (bf16[3,3,256,256]{3,2,1,0:T(8,128)(2,1)S(1)}, bf16[3,3,256,256]{3,2,1,0:T(8,128)(2,1)}, u32[]{:S(2)}) copy-start(bf16[3,3,256,256]{3,2,1,0:T(8,128)(2,1)} %param.21) | copy-start | bytes 3538948
  6.5 127.8 %all-gather.3.cloned.1.call-start = ((), (), s32[]{:S(2)}) async-start(), calls=%async_computation | async-start | bytes 4456448 | tf_op jit(solution)/shard_map/all_gather | solution.py:154
  8.3 14.0 %collective-permute-start = (bf16[4,1,128,48]{2,3,1,0:T(8,128)(2,1)S(1)}, bf16[4,1,128,48]{2,3,1,0:T(8,128)(2,1)S(1)}, u32[]{:S(2)}, u32[]{:S(2)}) collective-permute-start(bf16[4,1,128,48]{2,3,1,0:T(8,128)(2,1)S(1)} %get-tuple-element.28), channel_id=1, source_target_pairs={{0,1},{1,2},{2,3},{3,4},{4,5},{5,6},{6,7},{7,8},{8,9},{9,10},{10,1... | collective-permute-start | bytes 147464 | tf_op jit(solution)/shard_map/ppermute | solution.py:14
  13.3 9.0 %collective-permute-start.1 = (bf16[4,1,128,48]{2,3,1,0:T(8,128)(2,1)S(1)}, bf16[4,1,128,48]{2,3,1,0:T(8,128)(2,1)S(1)}, u32[]{:S(2)}, u32[]{:S(2)}) collective-permute-start(bf16[4,1,128,48]{2,3,1,0:T(8,128)(2,1)S(1)} %get-tuple-element.29), channel_id=1, source_target_pairs={{1,0},{2,1},{3,2},{4,3},{5,4},{6,5},{7,6},{8,7},{9,8},{10,9},{11,1... | collective-permute-start | bytes 147464 | tf_op jit(solution)/shard_map/ppermute | solution.py:17
  22.6 0.9 copy-start.3
  24.3 7.2 %copy-start.4 = (bf16[3,128,128]{2,1,0:T(8,128)(2,1)S(1)}, bf16[3,128,128]{2,1,0:T(8,128)(2,1)}, u32[]{:S(2)}) copy-start(bf16[3,128,128]{2,1,0:T(8,128)(2,1)} %param.16) | copy-start | bytes 294916
  24.3 7.0 %collective-permute-start.2 = (bf16[2,4,128,128]{3,2,1,0:T(8,128)(2,1)S(1)}, bf16[2,4,128,128]{3,2,1,0:T(8,128)(2,1)S(1)}, u32[]{:S(2)}, u32[]{:S(2)}) collective-permute-start(bf16[2,4,128,128]{3,2,1,0:T(8,128)(2,1)S(1)} %slice.252), channel_id=1, source_target_pairs={{0,32},{32,64},{64,96},{96,128},{128,160},{160,192},{192,224},{224... | collective-permute-start | bytes 786440 | tf_op jit(solution)/shard_map/ppermute | solution.py:25
  31.5 0.7 copy-start.8
  32.6 4.9 %collective-permute-start.3 = (bf16[4,1,128,128]{3,2,1,0:T(8,128)(2,1)S(1)}, bf16[4,1,128,128]{3,2,1,0:T(8,128)(2,1)S(1)}, u32[]{:S(2)}, u32[]{:S(2)}) collective-permute-start(bf16[4,1,128,128]{3,2,1,0:T(8,128)(2,1)S(1)} %slice.255), channel_id=1, source_target_pairs={{0,1},{1,2},{2,3},{3,4},{4,5},{5,6},{6,7},{7,8},{8,9},{9,10},{10,1... | collective-permute-start | bytes 393224 | tf_op jit(solution)/shard_map/ppermute | solution.py:25
  41.4 1.1 copy-start.6
  42.5 6.1 %copy-start.2 = (bf16[3,256,256]{2,1,0:T(8,128)(2,1)S(1)}, bf16[3,256,256]{2,1,0:T(8,128)(2,1)}, u32[]{:S(2)}) copy-start(bf16[3,256,256]{2,1,0:T(8,128)(2,1)} %param.19) | copy-start | bytes 1179652
  43.0 6.0 %copy-start.7 = (f32[256]{0:T(256)S(1)}, f32[256]{0:T(256)}, u32[]{:S(2)}) copy-start(f32[256]{0:T(256)} %param.20) | copy-start | bytes 3076
  43.0 5.4 %collective-permute-start.4 = (bf16[1,2,64,256]{3,2,1,0:T(8,128)(2,1)S(1)}, bf16[1,2,64,256]{3,2,1,0:T(8,128)(2,1)S(1)}, u32[]{:S(2)}, u32[]{:S(2)}) collective-permute-start(bf16[1,2,64,256]{3,2,1,0:T(8,128)(2,1)S(1)} %slice.256), channel_id=1, source_target_pairs={{0,32},{32,64},{64,96},{96,128},{128,160},{160,192},{192,224},{224... | collective-permute-start | bytes 196616 | tf_op jit(solution)/shard_map/ppermute | solution.py:25
  48.7 8.3 %copy-start.9 = (s32[16]{0:T(128)S(1)}, s32[16]{0:T(128)}, u32[]{:S(2)}) copy-start(s32[16]{0:T(128)} %param.14) | copy-start | bytes 196
  49.2 6.9 %collective-permute-start.5 = (bf16[2,2,64,256]{3,2,1,0:T(8,128)(2,1)S(1)}, bf16[2,2,64,256]{3,2,1,0:T(8,128)(2,1)S(1)}, u32[]{:S(2)}, u32[]{:S(2)}) collective-permute-start(bf16[2,2,64,256]{3,2,1,0:T(8,128)(2,1)S(1)} %bitcast.94), channel_id=1, source_target_pairs={{0,32},{32,64},{64,96},{96,128},{128,160},{160,192},{192,224},{224... | collective-permute-start | bytes 393224 | tf_op jit(solution)/shard_map/ppermute | solution.py:25
  144.2 6.0 %collective-permute-start.6 = (bf16[4,1,64,256]{3,2,1,0:T(8,128)(2,1)S(1)}, bf16[4,1,64,256]{3,2,1,0:T(8,128)(2,1)S(1)}, u32[]{:S(2)}, u32[]{:S(2)}) collective-permute-start(bf16[4,1,64,256]{3,2,1,0:T(8,128)(2,1)S(1)} %get-tuple-element.24), channel_id=1, source_target_pairs={{0,1},{1,2},{2,3},{3,4},{4,5},{5,6},{6,7},{7,8},{8,9},{9,10},{10,1... | collective-permute-start | bytes 393224 | tf_op jit(solution)/shard_map/ppermute | solution.py:14
  148.0 6.3 %collective-permute-start.7 = (bf16[4,1,64,256]{3,2,1,0:T(8,128)(2,1)S(1)}, bf16[4,1,64,256]{3,2,1,0:T(8,128)(2,1)S(1)}, u32[]{:S(2)}, u32[]{:S(2)}) collective-permute-start(bf16[4,1,64,256]{3,2,1,0:T(8,128)(2,1)S(1)} %get-tuple-element.25), channel_id=1, source_target_pairs={{1,0},{2,1},{3,2},{4,3},{5,4},{6,5},{7,6},{8,7},{9,8},{10,9},{11,1... | collective-permute-start | bytes 393224 | tf_op jit(solution)/shard_map/ppermute | solution.py:17
  154.9 1.0 copy-start.1
  155.7 0.7 copy-start.5
Sparse Core Ops, SparseCore 0:
  57.1 77.2 all-gather.2
where the time goes:
time: 165 us; the launch traced here: 164 us
  waiting for transfers between devices  92.2 us (56%)
  starting transfers between devices  27.8 us (17%)
  local copies, waits for them, and re-layouts  17.6 us (11%)
  between operations  14.7 us (9%)
  matrix products  7.75 us (5%)
  other arithmetic  4.09 us (2%)
    all_gather x1, waiting for transfers between devices, per_device(): lax.all_gather(flattened, 'tm', axis=0, tiled=True)  77.2 us
    ppermute x4, starting transfers between devices, passed_along(): return lax.ppermute(block, axis, route)  12.1 us
    ppermute x4, waiting for transfers between devices, passed_along(): return lax.ppermute(block, axis, route)  10.9 us
    unnamed x43, local copies, waits for them, and re-layouts  9.98 us
    ppermute x2, starting transfers between devices, padded_2(): lax.ppermute(lax.slice_in_dim(block, block.shape[dim] - width, None, axis...  8.68 us
    ppermute x2, starting transfers between devices, padded_2(): lax.ppermute(lax.slice_in_dim(block, 0, width, axis=dim), axis, backward)  7.06 us
    ppermute x2, waiting for transfers between devices, padded_2(): lax.ppermute(lax.slice_in_dim(block, 0, width, axis=dim), axis, backward)  4.05 us
    slice x9, local copies, waits for them, and re-layouts, spatial_conv(): padded[:, row_tap:row_tap + stride * out_rows:stride, col_tap:col_tap + s...  3.64 us
  transfers between devices with their start and end apart: 9, of which 6 were waited for; matrix products, arithmetic and copies ran while one was open for 3% of the time, Pallas kernels for 0%

commit v1 on v0

v1 whole, which is shorter than its diff:
```python
import functools

import jax
import jax.numpy as jnp
from jax import lax
from jax.experimental import pallas as pl
from jax.experimental.pallas import tpu as pltpu
from jax.sharding import PartitionSpec as P

MESH = pl.DeviceIdType.MESH
BF, F32 = jnp.bfloat16, jnp.float32

GROUPS = ((0, 0, 3), (1, 3, 3), (2, 6, 2), (3, 8, 3), (4, 11, 2))
PATCH = 768
STEP = 384


def iota(shape, dim):
    return lax.broadcasted_iota(jnp.int32, shape, dim)


def dot(a, b):
    return jnp.dot(a, b, preferred_element_type=F32)


def silu(v):
    return (0.5 * v) * (1.0 + jnp.tanh(0.5 * v))


def one_hot(row_key, col_key):
    return jnp.where(row_key == col_key, 1.0, 0.0).astype(BF)


def clip_of(frames, clip_ref, clips):
    total = jnp.zeros(frames.shape, jnp.int32)
    end = 0
    for k in range(clips):
        end = end + clip_ref[k]
        total = total + jnp.where(frames >= end, 1, 0)
    return total


def same_clip(key, tap, clip_ref, clips):
    same = clip_of(key, clip_ref, clips) == clip_of(tap, clip_ref, clips)
    return jnp.where(same & (tap >= 0), 1.0, 0.0)


def build_first_weights(win_ref, w1_ref):
    for g, (window, first, count) in enumerate(GROUPS):
        w1_ref[g] = jnp.zeros(w1_ref.shape[1:], BF)
        for a in range(3):
            for b in range(3):
                for n in range(count):
                    at = a * 256 + 48 * (first + n + b) - 128 * window
                    w1_ref[g, at : at + 48, n * 128 : (n + 1) * 128] = win_ref[a, b]


def build_temporal_weights(tin_ref, wt_ref):
    zero = jnp.zeros((128, 128), BF)
    blocks = (((0, None), (None, 2)), ((1, 0), (2, 1)))
    for part in range(2):
        for i in range(2):
            for j in range(2):
                k = blocks[part][i][j]
                wt_ref[part, i * 128 : (i + 1) * 128, j * 128 : (j + 1) * 128] = (
                    zero if k is None else tin_ref[k]
                )


def spread(recv_ref, x_ref, rel):
    row, col = iota((256, 256), 0), iota((256, 256), 1)
    perm = one_hot((row % 16) * 16 + ((row // 16) % 4) * 4 + row // 64, col)
    for half in range(2):
        lanes = slice(half * 384, half * 384 + 384)
        block = recv_ref[rel, :, :, lanes].reshape(256, 384)
        x_ref[4 * rel : 4 * rel + 4, :, :, lanes] = (
            dot(perm, block).astype(BF).reshape(4, 4, 16, 384)
        )


def first_spatial(x_ref, w1_ref, lt_ref, masks, row0, rows):
    for g, (window, first, count) in enumerate(GROUPS):
        lanes = slice(128 * window, 128 * window + 256)
        taps = [
            x_ref[pl.ds(row0 + a, rows), :, :, lanes].reshape(rows * 64, 256)
            for a in range(3)
        ]
        made = dot(jnp.concatenate(taps, axis=1), w1_ref[g, :, : count * 128])
        for n in range(count):
            s = made[:, n * 128 : (n + 1) * 128].reshape(rows, 4, 16, 128)
            late = s[:, 2:4].reshape(rows * 32, 128)
            late = pltpu.roll(late, 1, 0).reshape(rows, 2, 16, 128)
            at = (first + n, pl.ds(row0, rows))
            left, right = slice(0, 128), slice(128, 256)
            lt_ref[(0,) + at + (0, slice(None), left)] = (late[:, 0] * masks[0]).astype(BF)
            lt_ref[(0,) + at + (0, slice(None), right)] = s[:, 1].astype(BF)
            lt_ref[(1,) + at + (0, slice(None), left)] = (late[:, 1] * masks[1]).astype(BF)
            lt_ref[(1,) + at + (0, slice(None), right)] = s[:, 0].astype(BF)
            lt_ref[(0,) + at + (1, slice(None), left)] = (s[:, 0] * masks[2]).astype(BF)
            lt_ref[(0,) + at + (1, slice(None), right)] = s[:, 3].astype(BF)
            lt_ref[(1,) + at + (1, slice(None), left)] = (s[:, 1] * masks[3]).astype(BF)
            lt_ref[(1,) + at + (1, slice(None), right)] = s[:, 2].astype(BF)


def first_temporal(lt_ref, wt_ref, h1_ref, bias, pair_mask, col):
    one = dot(lt_ref[0, col].reshape(288, 256), wt_ref[0]).reshape(9, 2, 16, 256)
    two = dot(lt_ref[1, col].reshape(288, 256), wt_ref[1]).reshape(9, 2, 16, 256)
    early = one[..., :128] + two[..., :128] + bias
    late = one[..., 128:] + two[..., 128:] * pair_mask[None] + bias
    h1_ref[col % 2, col // 2, :, :, 0] = silu(early).astype(BF)
    h1_ref[col % 2, col // 2, :, :, 1] = silu(late).astype(BF)


def second(h1_ref, down_ref, tdown_ref, h2_ref, bias, masks, q):
    taps = [
        h1_ref[b % 2, b // 2 : b // 2 + 6, 2 * q + a].reshape(384, 128)
        for a in range(3)
        for b in range(3)
    ]
    s = dot(jnp.concatenate(taps, axis=1), down_ref[...].reshape(1152, 256))
    s = s.reshape(6, 2, 2, 16, 256)
    before = pltpu.roll(s[:, 1, 1].reshape(96, 256), 1, 0).reshape(6, 1, 16, 256)
    k0 = jnp.concatenate([before, s[:, 0:1, 1]], axis=1) * masks[0]
    k1 = s[:, :, 0] * masks[1]
    k2 = s[:, :, 1]
    taps = jnp.concatenate(
        [k.astype(BF).reshape(192, 256) for k in (k0, k1, k2)], axis=1
    )
    made = dot(taps, tdown_ref[...].reshape(768, 256)) + bias
    h2_ref[q] = silu(made).astype(BF).reshape(6, 2, 16, 256)


def third(h2_ref, wout_ref, tout_ref, bias, masks):
    taps = [
        h2_ref[a : a + 2, b : b + 4].reshape(256, 256) for a in range(3) for b in range(3)
    ]
    s = dot(jnp.concatenate(taps, axis=1), wout_ref[...].reshape(2304, 256))
    before = pltpu.roll(s, 1, 0).reshape(8, 2, 16, 256)
    s = s.reshape(8, 2, 16, 256)
    k0 = before * masks[0]
    k1 = jnp.concatenate([before[:, 1:2], s[:, 0:1]], axis=1) * masks[1]
    taps = jnp.concatenate([k.astype(BF).reshape(256, 256) for k in (k0, k1, s)], axis=1)
    return (dot(taps, tout_ref[...].reshape(768, 256)) + bias).astype(BF)


def local_part(
    clips, at_left, at_right, at_top, at_bottom, clip_ref, recv_ref, x_ref, w1_ref, lt_ref,
    wt_ref, h1_ref, h2_ref, down_ref, tdown_ref, wout_ref, tout_ref, bin_ref, bdown_ref, bout_ref,
):
    for rel in range(3):
        spread(recv_ref, x_ref, rel)
    base = 4 * iota((16, 128), 0)
    check = functools.partial(same_clip, clip_ref=clip_ref, clips=clips)
    masks = [check(base, base - 2), check(base, base - 1), check(base + 2, base), check(base + 2, base + 1)]
    pair_mask = jnp.stack([check(base + 1, base), check(base + 3, base + 2)])

    def rows_of(i, carry):
        first_spatial(x_ref, w1_ref, lt_ref, masks, 3 * i, 3)
        return carry

    lax.fori_loop(0, 3, rows_of, 0)
    bias_in = bin_ref[...]

    def column(i, carry):
        first_temporal(lt_ref, wt_ref, h1_ref, bias_in, pair_mask, i)
        return carry

    lax.fori_loop(0, 13, column, 0)

    @pl.when(at_top)
    def _():
        h1_ref[:, :, 2] = jnp.zeros((2, 7, 2, 2, 16, 128), BF)

    @pl.when(at_left)
    def _():
        h1_ref[0, 1] = jnp.zeros((9, 2, 2, 16, 128), BF)

    base = 4 * iota((2, 16, 256), 1) + 2 * iota((2, 16, 256), 0)
    masks = [check(base + 1, base - 1), check(base + 1, base)]
    bias_down = bdown_ref[...]

    def reduced_row(i, carry):
        second(h1_ref, down_ref, tdown_ref, h2_ref, bias_down, masks, i)
        return carry

    lax.fori_loop(0, 4, reduced_row, 0)

    @pl.when(at_top)
    def _():
        h2_ref[0] = jnp.zeros((6, 2, 16, 256), BF)

    @pl.when(at_bottom)
    def _():
        h2_ref[3] = jnp.zeros((6, 2, 16, 256), BF)

    @pl.when(at_left)
    def _():
        h2_ref[:, 0] = jnp.zeros((4, 2, 16, 256), BF)

    @pl.when(at_right)
    def _():
        h2_ref[:, 5] = jnp.zeros((4, 2, 16, 256), BF)

    masks = [check(base + 1, base - 3), check(base + 1, base - 1)]
    return third(h2_ref, wout_ref, tout_ref, bout_ref[...], masks)


def kernel(
    clips,
    x_ref, clip_ref, owner_ref, win_ref, tin_ref, bin_ref, down_hbm, tdown_hbm, bdown_ref, wout_hbm, tout_hbm, bout_ref,
    out_ref,
    xpad, recv, xs, w1, lt, wt, h1, h2, down, tdown, wout, tout, parts, landed,
    weight_sem, own_sem, send_sem, recv_sem, fsend_sem, frecv_sem, send2_sem, recv2_sem,
):
    me, row = lax.axis_index("tm"), lax.axis_index("tile")
    n, n_rows = lax.axis_size("tm"), lax.axis_size("tile")
    at_top, at_bottom = row == 0, row == n_rows - 1
    barrier = pltpu.get_barrier_semaphore()
    for k in range(1, n):
        pl.semaphore_signal(barrier, inc=1, device_id={"tm": lax.rem(me + k, n)}, device_id_type=MESH)

    @pl.when(jnp.logical_not(at_top))
    def _():
        pl.semaphore_signal(barrier, inc=1, device_id={"tile": row - 1}, device_id_type=MESH)

    @pl.when(jnp.logical_not(at_bottom))
    def _():
        pl.semaphore_signal(barrier, inc=1, device_id={"tile": row + 1}, device_id_type=MESH)

    loads = [
        pltpu.make_async_copy(source, target, weight_sem.at[i])
        for i, (source, target) in enumerate(
            ((down_hbm, down), (tdown_hbm, tdown), (wout_hbm, wout), (tout_hbm, tout))
        )
    ]
    for load in loads:
        load.start()
    mine = jnp.concatenate([x_ref[f].astype(F32) for f in range(4)], axis=0)
    side = jnp.zeros((16, 192), F32)
    xpad[...] = jnp.concatenate([side, mine, side], axis=1).astype(BF)
    pl.semaphore_wait(barrier, n - 1 + jnp.where(at_top, 0, 1) + jnp.where(at_bottom, 0, 1))

    def patch(who):
        return xpad.at[:, pl.ds(pl.multiple_of(who * STEP, 128), PATCH)]

    def sent(k):
        to = lax.rem(me + k, n)
        return pltpu.make_async_remote_copy(
            src_ref=patch(to), dst_ref=recv.at[1, me], send_sem=send_sem.at[k], recv_sem=recv_sem.at[me],
            device_id={"tm": to}, device_id_type=MESH,
        )

    def arriving(k):
        source = lax.rem(me - k + n, n)
        return pltpu.make_async_remote_copy(
            src_ref=patch(me), dst_ref=recv.at[1, source], send_sem=send_sem.at[k], recv_sem=recv_sem.at[source],
            device_id={"tm": source}, device_id_type=MESH,
        )

    def passed(source, down_way):
        way, to = (0, row + 1) if down_way else (1, row - 1)
        return pltpu.make_async_remote_copy(
            src_ref=recv.at[1, source], dst_ref=recv.at[2 * way, source], send_sem=fsend_sem.at[way, source],
            recv_sem=frecv_sem.at[way, source], device_id={"tile": to}, device_id_type=MESH,
        )

    def pass_on(source):
        @pl.when(jnp.logical_not(at_bottom))
        def _():
            passed(source, True).start()

        @pl.when(jnp.logical_not(at_top))
        def _():
            passed(source, False).start()

    def start_send(k, carry):
        sent(k).start()
        return carry

    lax.fori_loop(1, n, start_send, 0)
    own = pltpu.make_async_copy(patch(me), recv.at[1, me], own_sem)
    own.start()
    own.wait()
    pass_on(me)
    build_first_weights(win_ref, w1)
    build_temporal_weights(tin_ref, wt)

    @pl.when(at_top)
    def _():
        recv[0] = jnp.zeros(recv.shape[1:], BF)

    @pl.when(at_bottom)
    def _():
        recv[2] = jnp.zeros(recv.shape[1:], BF)

    def relay(k, carry):
        arriving(k).wait_recv()
        pass_on(lax.rem(me - k + n, n))
        return carry

    lax.fori_loop(1, n, relay, 0)

    def settle(k, carry):
        @pl.when(jnp.logical_not(at_top))
        def _():
            passed(k, True).wait_recv()
            passed(k, False).wait_send()

        @pl.when(jnp.logical_not(at_bottom))
        def _():
            passed(k, False).wait_recv()
            passed(k, True).wait_send()

        return carry

    lax.fori_loop(0, n, settle, 0)
    for load in loads:
        load.wait()
    encoded = local_part(
        clips, me == 0, me == n - 1, at_top, at_bottom, clip_ref, recv, xs, w1, lt,
        wt, h1, h2, down, tdown, wout, tout, bin_ref, bdown_ref, bout_ref,
    )
    r, c = iota((256, 256), 0), iota((256, 256), 1)
    owner = jnp.zeros((256, 256), jnp.int32)
    for k in range(n):
        owner = owner + jnp.where(c % 16 == k, owner_ref[k], 0)
    spot = ((c // 16) % 2) * 8 + c // 32
    parts[...] = dot(one_hot(r, owner * 16 + spot), encoded).astype(BF).reshape(16, 16, 256)

    def part_to(k):
        to = lax.rem(me + k, n)
        return pltpu.make_async_remote_copy(
            src_ref=parts.at[to], dst_ref=landed.at[me], send_sem=send2_sem.at[k], recv_sem=recv2_sem.at[me],
            device_id={"tm": to}, device_id_type=MESH,
        )

    def part_from(k):
        source = lax.rem(me - k + n, n)
        return pltpu.make_async_remote_copy(
            src_ref=parts.at[me], dst_ref=landed.at[source], send_sem=send2_sem.at[k], recv_sem=recv2_sem.at[source],
            device_id={"tm": source}, device_id_type=MESH,
        )

    def start_part(k, carry):
        part_to(k).start()
        return carry

    lax.fori_loop(1, n, start_part, 0)
    own = pltpu.make_async_copy(parts.at[me], landed.at[me], own_sem)
    own.start()
    own.wait()

    def end(k, carry):
        sent(k).wait_send()
        part_to(k).wait_send()
        part_from(k).wait_recv()
        return carry

    lax.fori_loop(1, n, end, 0)
    perm = one_hot(((r // 4) % 16) * 16 + (r // 64) * 4 + r % 4, c)
    out_ref[...] = dot(perm, landed[...].reshape(256, 256)).astype(BF).reshape(2, 2, 64, 256)


def per_device(
    haar_video, clip_lengths, block_owner, spatial_in, temporal_in, bias_in, spatial_down, temporal_down, bias_down,
    spatial_out, temporal_out, bias_out,
):
    clips = clip_lengths.shape[0]
    vmem, smem, hbm = (
        pl.BlockSpec(memory_space=pltpu.VMEM),
        pl.BlockSpec(memory_space=pltpu.SMEM),
        pl.BlockSpec(memory_space=pl.ANY),
    )
    dma = pltpu.SemaphoreType.DMA
    return pl.pallas_call(
        functools.partial(kernel, clips),
        out_shape=jax.ShapeDtypeStruct((2, 2, 64, 256), BF),
        in_specs=[vmem, smem, smem, vmem, vmem, vmem, hbm, hbm, vmem, hbm, hbm, vmem],
        out_specs=vmem,
        scratch_shapes=[
            pltpu.VMEM((16, 6528), BF),
            pltpu.VMEM((3, 16, 16, PATCH), BF),
            pltpu.VMEM((12, 4, 16, PATCH), BF),
            pltpu.VMEM((5, 768, 384), BF),
            pltpu.VMEM((2, 13, 9, 2, 16, 256), BF),
            pltpu.VMEM((2, 256, 256), BF),
            pltpu.VMEM((2, 7, 9, 2, 2, 16, 128), BF),
            pltpu.VMEM((4, 6, 2, 16, 256), BF),
            pltpu.VMEM(spatial_down.shape, BF),
            pltpu.VMEM(temporal_down.shape, BF),
            pltpu.VMEM(spatial_out.shape, BF),
            pltpu.VMEM(temporal_out.shape, BF),
            pltpu.VMEM((16, 16, 256), BF),
            pltpu.VMEM((16, 16, 256), BF),
            dma((4,)),
            dma,
            dma((16,)),
            dma((16,)),
            dma((2, 16)),
            dma((2, 16)),
            dma((16,)),
            dma((16,)),
        ],
        compiler_params=pltpu.CompilerParams(
            collective_id=0, has_side_effects=True, vmem_limit_bytes=62 * 2**20
        ),
    )(
        haar_video, clip_lengths, block_owner, spatial_in, temporal_in, bias_in.reshape(1, 128), spatial_down,
        temporal_down, bias_down.reshape(1, 256), spatial_out, temporal_out, bias_out.reshape(1, 256),
    )


def solution(mesh):
    placed = (P("tm", "tile", None), P(), P(), P(), P(), P(), P(), P(), P(), P(), P(), P())
    return jax.shard_map(
        per_device,
        mesh=mesh,
        in_specs=placed,
        out_specs=P("tm", "tile", None, None),
        check_vma=False,
    )
```

time: 165 us -> 40 us (0.24)
  waiting for transfers between devices: 92.2 us -> 0 us
  Pallas kernels: 0 us -> 37.9 us
  starting transfers between devices: 27.8 us -> 0 us
  local copies, waits for them, and re-layouts: 17.6 us -> 1.57 us
  between operations: 14.7 us -> 0.01 us
  matrix products: 7.75 us -> 0 us
  other arithmetic: 4.09 us -> 0 us
    all_gather x1 -> x0, waiting for transfers between devices: 77.2 us -> none  [per_device(): lax.all_gather(flattened, 'tm', axis=0, tiled=True)]
    pallas_call x0 -> x1, Pallas kernels: none -> 37.9 us  [per_device(): pl.pallas_call(functools.partial(kernel, clips), out_shape=jax.ShapeDtype...]
    ppermute x8 -> x0, starting transfers between devices: 27.8 us -> none  [the longest x4 12.1 us: passed_along(): return lax.ppermute(block, axis, route)]
    ppermute x8 -> x0, waiting for transfers between devices: 15 us -> none  [the longest x4 10.9 us: passed_along(): return lax.ppermute(block, axis, route)]
    unnamed x43 -> x1, local copies, waits for them, and re-layouts: 9.98 us -> 1.57 us
    dot_general x13 -> x0, matrix products: 7.75 us -> none  [the longest x1 2.84 us: pick_rows(): return jnp.dot(select, shard_piece, preferred_element_type=jnp.float32)]
    slice x17 -> x0, local copies, waits for them, and re-layouts: 4.37 us -> none  [the longest x9 3.64 us: spatial_conv(): padded[:, row_tap:row_tap + stride * out_rows:stride, col_tap:col_tap + s...]
    reduce_sum x6 -> x0, other arithmetic: 2.18 us -> none  [the longest x1 1.3 us: per_device(): source_block = jnp.sum(jnp.where(block_owner == my_index, slot_ids, 0))]
  transfers between devices with their start and end apart: 9 -> 0, of which waited for: 6 -> 0; matrix products, arithmetic and copies ran while one was open for 3% -> 0% of each run, Pallas kernels for 0% -> 0%
where the time goes in v1:
time: 40 us; the launch traced here: 39.4 us
  Pallas kernels  37.9 us (95%)
  local copies, waits for them, and re-layouts  1.57 us (4%)
    pallas_call x1, Pallas kernels, per_device(): pl.pallas_call(functools.partial(kernel, clips), out_shape=jax.ShapeDtype...  37.9 us
    unnamed x1, local copies, waits for them, and re-layouts  1.57 us

profile of v1, /device:TPU:1, one launch (start us, length us, event | category | flops | bytes accessed | tf_op | source)
XLA Modules:
  0.0 39.4 jit_solution(5322950978184580964)
XLA Ops:
  0.0 37.9 %shard_map.118 = bf16[2,2,64,256]{3,2,1,0:T(8,128)(2,1)} custom-call(bf16[4,4,6144]{2,1,0:T(4,128)(2,1)} %x_ref.1, s32[16]{0:T(128)} %clip_ref.1, s32[16]{0:T(128)} %owner_ref.1, bf16[3,3,48,128]{3,2,1,0:T(8,128)(2,1)} %win_ref.1, bf16[3,128,128]{2,1,0:T(8,128)(2,1)} %tin_ref.1, f32[1,128]{1,0:T(1,128)} %bitcast.5, bf16[3,3,128,256]{3,2,1,0:T(8,128)(2,1)} %down_hbm.1, ...), custom_call_target="tpu_custom_call" | custom-call | tf_op jit(solution)/shard_map/pallas_call | solution.py:375
  37.9 1.6 %copy.14 = bf16[2,2,64,256]{3,2,1,0:T(8,128)(2,1)} copy(bf16[2,2,64,256]{3,2,1,0:T(8,128)(2,1)} %shard_map.118) | data formatting | bytes 262144

commit v2 on v1

v2 whole, which is shorter than its diff:
```python
import functools

import jax
import jax.numpy as jnp
from jax import lax
from jax.experimental import pallas as pl
from jax.experimental.pallas import tpu as pltpu
from jax.sharding import PartitionSpec as P

MESH = pl.DeviceIdType.MESH
BF, F32 = jnp.bfloat16, jnp.float32

GROUPS = ((0, 0, 3), (1, 3, 3), (2, 6, 2), (3, 8, 3), (4, 11, 2))
PATCH = 768
STEP = 384


def iota(shape, dim):
    return lax.broadcasted_iota(jnp.int32, shape, dim)


def dot(a, b):
    return jnp.dot(a, b, preferred_element_type=F32)


def silu(v):
    return (0.5 * v) * (1.0 + jnp.tanh(0.5 * v))


def one_hot(row_key, col_key):
    return jnp.where(row_key == col_key, 1.0, 0.0).astype(BF)


def clip_masks(clip_ref, clips):
    base = 4 * iota((16, 128), 0)
    ends, end = [], 0
    for k in range(clips):
        end = end + clip_ref[k]
        ends.append(end)
    ids = {}
    for i in range(-3, 4):
        ids[i] = sum(jnp.where(base + i >= e, 1, 0) for e in ends)

    def same(key, tap):
        return jnp.where((ids[key] == ids[tap]) & (base + tap >= 0), 1.0, 0.0)

    return same


def build_first_weights(win_ref, w1_ref):
    for g, (window, first, count) in enumerate(GROUPS):
        w1_ref[g] = jnp.zeros(w1_ref.shape[1:], BF)
        for a in range(3):
            for b in range(3):
                for n in range(count):
                    at = a * 256 + 48 * (first + n + b) - 128 * window
                    w1_ref[g, at : at + 48, n * 128 : (n + 1) * 128] = win_ref[a, b]


def build_temporal_weights(tin_ref, wt_ref):
    zero = jnp.zeros((128, 128), BF)
    blocks = (((0, None), (None, 2)), ((1, 0), (2, 1)))
    for part in range(2):
        for i in range(2):
            for j in range(2):
                k = blocks[part][i][j]
                wt_ref[part, i * 128 : (i + 1) * 128, j * 128 : (j + 1) * 128] = (
                    zero if k is None else tin_ref[k]
                )


def spread(recv_ref, x_ref, rel):
    row, col = iota((256, 256), 0), iota((256, 256), 1)
    perm = one_hot((row % 16) * 16 + ((row // 16) % 4) * 4 + row // 64, col)
    for half in range(2):
        lanes = slice(half * 384, half * 384 + 384)
        block = recv_ref[rel, :, :, lanes].reshape(256, 384)
        x_ref[pl.ds(4 * rel, 4), :, :, lanes] = (
            dot(perm, block).astype(BF).reshape(4, 4, 16, 384)
        )


def first_spatial(x_ref, w1_ref, lt_ref, masks, row0, rows):
    left, right = slice(0, 128), slice(128, 256)
    for g, (window, first, count) in enumerate(GROUPS):
        lanes = slice(128 * window, 128 * window + 256)
        taps = [
            x_ref[pl.ds(row0 + a, rows), :, :, lanes].reshape(rows * 64, 256)
            for a in range(3)
        ]
        made = dot(jnp.concatenate(taps, axis=1), w1_ref[g, :, : count * 128])
        for n in range(count):
            s = made[:, n * 128 : (n + 1) * 128].reshape(rows, 4, 16, 128)
            late = s[:, 2:4].reshape(rows * 32, 128)
            late = pltpu.roll(late, 1, 0).reshape(rows, 2, 16, 128)

            def put(part, pair, lanes, value):
                lt_ref[part, first + n, pl.ds(row0, rows), pair, :, lanes] = value.astype(BF)

            put(0, 0, left, late[:, 0] * masks[0])
            put(0, 0, right, s[:, 1])
            put(1, 0, left, late[:, 1] * masks[1])
            put(1, 0, right, s[:, 0])
            put(0, 1, left, s[:, 0] * masks[2])
            put(0, 1, right, s[:, 3])
            put(1, 1, left, s[:, 1] * masks[3])
            put(1, 1, right, s[:, 2])


def first_temporal(lt_ref, wt_ref, h1_ref, bias, pair_mask, row0, rows):
    for col in range(13):
        one, two = (
            dot(lt_ref[i, col, pl.ds(row0, rows)].reshape(rows * 32, 256), wt_ref[i]).reshape(rows, 2, 16, 256)
            for i in range(2)
        )
        early = one[..., :128] + two[..., :128] + bias
        late = one[..., 128:] + two[..., 128:] * pair_mask[None] + bias
        h1_ref[col % 2, col // 2, pl.ds(row0, rows), :, 0] = silu(early).astype(BF)
        h1_ref[col % 2, col // 2, pl.ds(row0, rows), :, 1] = silu(late).astype(BF)


def second(h1_ref, down_ref, tdown_ref, h2_ref, bias, masks, q):
    taps = [
        h1_ref[b % 2, b // 2 : b // 2 + 6, 2 * q + a].reshape(384, 128)
        for a in range(3)
        for b in range(3)
    ]
    s = dot(jnp.concatenate(taps, axis=1), down_ref[...].reshape(1152, 256))
    s = s.reshape(6, 2, 2, 16, 256)
    before = pltpu.roll(s[:, 1, 1].reshape(96, 256), 1, 0).reshape(6, 1, 16, 256)
    k0 = jnp.concatenate([before, s[:, 0:1, 1]], axis=1) * masks[0]
    k1 = s[:, :, 0] * masks[1]
    k2 = s[:, :, 1]
    taps = jnp.concatenate([k.astype(BF).reshape(192, 256) for k in (k0, k1, k2)], axis=1)
    made = dot(taps, tdown_ref[...].reshape(768, 256)) + bias
    h2_ref[q] = silu(made).astype(BF).reshape(6, 2, 16, 256)


def third(h2_ref, wout_ref, tout_ref, bias, masks):
    taps = [
        h2_ref[a : a + 2, b : b + 4].reshape(256, 256) for a in range(3) for b in range(3)
    ]
    s = dot(jnp.concatenate(taps, axis=1), wout_ref[...].reshape(2304, 256))
    before = pltpu.roll(s, 1, 0).reshape(8, 2, 16, 256)
    s = s.reshape(8, 2, 16, 256)
    k0 = before * masks[0]
    k1 = jnp.concatenate([before[:, 1:2], s[:, 0:1]], axis=1) * masks[1]
    taps = jnp.concatenate([k.astype(BF).reshape(256, 256) for k in (k0, k1, s)], axis=1)
    return (dot(taps, tout_ref[...].reshape(768, 256)) + bias).astype(BF)


OFFSETS = sorted(
    ((dx, dy) for dx in range(4) for dy in range(4) if dx or dy),
    key=lambda o: (-min(o[0], 4 - o[0]) - min(o[1], 4 - o[1]), o),
)


def kernel(
    clips,
    x_hbm, clip_hbm, owner_hbm, win_hbm, tin_hbm, bin_hbm, down_hbm, tdown_hbm, bdown_hbm, wout_hbm, tout_hbm, bout_hbm,
    landed,
    x_in, clip_ref, owner_ref, win_ref, tin_ref, bin_ref, down, tdown, bdown_ref, wout, tout, bout_ref,
    xpad, recv, xs, w1, lt, wt, h1, h2, parts,
    load_sem, own_sem, send_sem, recv_sem, fsend_sem, frecv_sem, send2_sem, recv2_sem,
):
    me, row = lax.axis_index("tm"), lax.axis_index("tile")
    n, n_rows = lax.axis_size("tm"), lax.axis_size("tile")
    core = lax.rem(row, 2)
    at_top, at_bottom = row == 0, row == n_rows - 1
    barrier = pltpu.get_barrier_semaphore()

    def beside(dx, dy):
        return lax.rem(me // 4 + dx, 4) * 4 + lax.rem(lax.rem(me, 4) + dy, 4)

    for o in OFFSETS:
        pl.semaphore_signal(barrier, inc=1, device_id={"tm": beside(*o)}, device_id_type=MESH)

    @pl.when(jnp.logical_not(at_top))
    def _():
        pl.semaphore_signal(barrier, inc=1, device_id={"tile": row - 1}, device_id_type=MESH)

    @pl.when(jnp.logical_not(at_bottom))
    def _():
        pl.semaphore_signal(barrier, inc=1, device_id={"tile": row + 1}, device_id_type=MESH)

    x_load, *loads = [
        pltpu.make_async_copy(source, target, load_sem.at[i])
        for i, (source, target) in enumerate(
            (
                (x_hbm, x_in), (clip_hbm, clip_ref), (owner_hbm, owner_ref), (win_hbm, win_ref), (tin_hbm, tin_ref),
                (bin_hbm, bin_ref), (bdown_hbm, bdown_ref), (bout_hbm, bout_ref), (down_hbm, down),
                (tdown_hbm, tdown), (wout_hbm, wout), (tout_hbm, tout),
            )
        )
    ]
    x_load.start()
    for load in loads:
        load.start()
    x_load.wait()
    mine = jnp.concatenate([x_in[f].astype(F32) for f in range(4)], axis=0)
    side = jnp.zeros((16, 192), F32)
    xpad[...] = jnp.concatenate([side, mine, side], axis=1).astype(BF)
    pl.semaphore_wait(barrier, n - 1 + jnp.where(at_top, 0, 1) + jnp.where(at_bottom, 0, 1))

    def patch(who):
        return xpad.at[:, pl.ds(pl.multiple_of(who * STEP, 128), PATCH)]

    def across(i, o, source, target, send, recv_):
        to = beside(*o)
        return pltpu.make_async_remote_copy(
            src_ref=source(to), dst_ref=target(me), send_sem=send.at[i], recv_sem=recv_.at[me],
            device_id={"tm": to}, device_id_type=MESH,
        )

    def from_across(i, o, source, target, send, recv_):
        other = beside(-o[0] % 4, -o[1] % 4)
        return other, pltpu.make_async_remote_copy(
            src_ref=source(me), dst_ref=target(other), send_sem=send.at[i], recv_sem=recv_.at[other],
            device_id={"tm": other}, device_id_type=MESH,
        )

    out_way = (patch, lambda who: recv.at[1, who], send_sem, recv_sem)
    back_way = (lambda who: parts.at[who], lambda who: landed.at[who], send2_sem, recv2_sem)

    def passed(source, way):
        to = row + 1 - 2 * way
        return pltpu.make_async_remote_copy(
            src_ref=recv.at[1, source], dst_ref=recv.at[2 * way, source], send_sem=fsend_sem.at[way, source],
            recv_sem=frecv_sem.at[way, source], device_id={"tile": to}, device_id_type=MESH,
        )

    far_up, far_down = jnp.logical_and(core == 0, jnp.logical_not(at_top)), jnp.logical_and(core == 1, jnp.logical_not(at_bottom))

    def pass_on(source):
        @pl.when(jnp.logical_or(far_up, far_down))
        def _():
            passed(source, 1 - core).start()

        passed(source, core).start()

    for i, o in enumerate(OFFSETS):
        across(i, o, *out_way).start()
    own = pltpu.make_async_copy(patch(me), recv.at[1, me], own_sem)
    own.start()
    own.wait()
    pass_on(me)
    for load in loads[:7]:
        load.wait()
    build_first_weights(win_ref, w1)
    build_temporal_weights(tin_ref, wt)
    same = clip_masks(clip_ref, clips)
    bias_in, bias_down = bin_ref[...], bdown_ref[...]
    first_masks = [same(0, -2), same(0, -1), same(2, 0), same(2, 1)]
    pair_mask = jnp.stack([same(1, 0), same(3, 2)])

    def wide(one, two):
        both = jnp.stack([one, two])
        return jnp.concatenate([both, both], axis=2)

    second_masks = [wide(same(1, -1), same(3, 1)), wide(same(1, 0), same(3, 2))]
    third_masks = [wide(same(1, -3), same(3, -1)), wide(same(1, -1), same(3, 1))]

    @pl.when(at_top)
    def _():
        recv[0] = jnp.zeros(recv.shape[1:], BF)

    @pl.when(at_bottom)
    def _():
        recv[2] = jnp.zeros(recv.shape[1:], BF)

    for i, o in enumerate(OFFSETS):
        other, copy = from_across(i, o, *out_way)
        copy.wait_recv()
        pass_on(other)
    for load in loads[7:]:
        load.wait()
    spread(recv, xs, 1)

    def near(k, carry):
        passed(k, 1 - core).wait_recv()
        return carry

    lax.fori_loop(0, n, near, 0)
    spread(recv, xs, 2 * (1 - core))

    def section_one(row0, rows):
        first_spatial(xs, w1, lt, first_masks, row0, rows)
        first_temporal(lt, wt, h1, bias_in, pair_mask, row0, rows)

    def clear_left_one():
        @pl.when(me == 0)
        def _():
            h1[0, 1] = jnp.zeros((9, 2, 2, 16, 128), BF)

    section_one(4 * (1 - core), 5)
    clear_left_one()
    for q in range(2):
        second(h1, down, tdown, h2, bias_down, second_masks, 2 * (1 - core) + q)

    @pl.when(jnp.logical_or(far_up, far_down))
    def _():
        def far(k, carry):
            passed(k, core).wait_recv()
            return carry

        lax.fori_loop(0, n, far, 0)

    spread(recv, xs, 2 * core)
    section_one(5 * core, 4)
    clear_left_one()

    @pl.when(at_top)
    def _():
        h1[:, :, 2] = jnp.zeros((2, 7, 2, 2, 16, 128), BF)

    for q in range(2):
        second(h1, down, tdown, h2, bias_down, second_masks, 2 * core + q)

    @pl.when(at_top)
    def _():
        h2[0] = jnp.zeros((6, 2, 16, 256), BF)

    @pl.when(at_bottom)
    def _():
        h2[3] = jnp.zeros((6, 2, 16, 256), BF)

    @pl.when(me == 0)
    def _():
        h2[:, 0] = jnp.zeros((4, 2, 16, 256), BF)

    @pl.when(me == n - 1)
    def _():
        h2[:, 5] = jnp.zeros((4, 2, 16, 256), BF)

    encoded = third(h2, wout, tout, bout_ref[...], third_masks)
    r, c = iota((256, 256), 0), iota((256, 256), 1)
    owner = jnp.zeros((8, 256), jnp.int32)
    for k in range(n):
        owner = owner + jnp.where(iota((8, 256), 1) % 16 == k, owner_ref[k], 0)
    spot = ((c // 16) % 2) * 8 + c // 32
    parts[...] = dot(one_hot(r, owner[:1] * 16 + spot), encoded).astype(BF).reshape(16, 16, 256)
    for i, o in enumerate(OFFSETS):
        across(i, o, *back_way).start()
    own = pltpu.make_async_copy(parts.at[me], landed.at[me], own_sem)
    own.start()
    own.wait()
    for i, o in enumerate(OFFSETS):
        across(i, o, *out_way).wait_send()

    def settle(k, carry):
        passed(k, core).wait_send()
        return carry

    lax.fori_loop(0, n, settle, 0)

    @pl.when(jnp.logical_or(far_up, far_down))
    def _():
        def settle_far(k, carry):
            passed(k, 1 - core).wait_send()
            return carry

        lax.fori_loop(0, n, settle_far, 0)

    for i, o in enumerate(OFFSETS):
        across(i, o, *back_way).wait_send()
        from_across(i, o, *back_way)[1].wait_recv()


def lay_out(landed, out_ref):
    r, c = iota((256, 256), 0), iota((256, 256), 1)
    perm = one_hot(((r // 4) % 16) * 16 + (r // 64) * 4 + r % 4, c)
    out_ref[...] = dot(perm, landed[...].reshape(256, 256)).astype(BF).reshape(2, 2, 64, 256)


def per_device(
    haar_video, clip_lengths, block_owner, spatial_in, temporal_in, bias_in, spatial_down, temporal_down, bias_down,
    spatial_out, temporal_out, bias_out,
):
    clips = clip_lengths.shape[0]
    vmem, hbm = pl.BlockSpec(memory_space=pltpu.VMEM), pl.BlockSpec(memory_space=pl.ANY)
    dma = pltpu.SemaphoreType.DMA
    landed = pl.pallas_call(
        functools.partial(kernel, clips),
        out_shape=jax.ShapeDtypeStruct((16, 16, 256), BF),
        in_specs=[hbm] * 12,
        out_specs=vmem,
        scratch_shapes=[
            pltpu.VMEM(haar_video.shape, BF),
            pltpu.SMEM(clip_lengths.shape, jnp.int32),
            pltpu.SMEM(block_owner.shape, jnp.int32),
            pltpu.VMEM(spatial_in.shape, BF),
            pltpu.VMEM(temporal_in.shape, BF),
            pltpu.VMEM((1, 128), F32),
            pltpu.VMEM(spatial_down.shape, BF),
            pltpu.VMEM(temporal_down.shape, BF),
            pltpu.VMEM((1, 256), F32),
            pltpu.VMEM(spatial_out.shape, BF),
            pltpu.VMEM(temporal_out.shape, BF),
            pltpu.VMEM((1, 256), F32),
            pltpu.VMEM((16, 6528), BF),
            pltpu.VMEM((3, 16, 16, PATCH), BF),
            pltpu.VMEM((12, 4, 16, PATCH), BF),
            pltpu.VMEM((5, 768, 384), BF),
            pltpu.VMEM((2, 13, 9, 2, 16, 256), BF),
            pltpu.VMEM((2, 256, 256), BF),
            pltpu.VMEM((2, 7, 9, 2, 2, 16, 128), BF),
            pltpu.VMEM((4, 6, 2, 16, 256), BF),
            pltpu.VMEM((16, 16, 256), BF),
            dma((12,)),
            dma,
            dma((15,)),
            dma((16,)),
            dma((2, 16)),
            dma((2, 16)),
            dma((15,)),
            dma((16,)),
        ],
        compiler_params=pltpu.CompilerParams(
            collective_id=0, has_side_effects=True, vmem_limit_bytes=62 * 2**20
        ),
    )(
        haar_video, clip_lengths, block_owner, spatial_in, temporal_in, bias_in.reshape(1, 128), spatial_down,
        temporal_down, bias_down.reshape(1, 256), spatial_out, temporal_out, bias_out.reshape(1, 256),
    )
    return pl.pallas_call(
        lay_out,
        out_shape=jax.ShapeDtypeStruct((2, 2, 64, 256), BF),
        in_specs=[vmem],
        out_specs=vmem,
    )(landed)


def solution(mesh):
    placed = (P("tm", "tile", None), P(), P(), P(), P(), P(), P(), P(), P(), P(), P(), P())
    return jax.shard_map(
        per_device,
        mesh=mesh,
        in_specs=placed,
        out_specs=P("tm", "tile", None, None),
        check_vma=False,
    )
```

time: 40 us -> 33.1 us (0.83); the launches traced: 39.4 us -> 33 us
  Pallas kernels: 37.9 us -> 32.9 us
  local copies, waits for them, and re-layouts: 1.57 us -> 0 us
    pallas_call x1, Pallas kernels: 37.9 us -> 31.2 us  [per_device(): pl.pallas_call(functools.partial(kernel, clips), out_shape=jax.ShapeDtype...]
    pallas_call x0 -> x1, Pallas kernels: none -> 1.75 us  [per_device(): pl.pallas_call(lay_out, out_shape=jax.ShapeDtypeStruct((2, 2, 64, 256), B...]
    unnamed x1 -> x0, local copies, waits for them, and re-layouts: 1.57 us -> none
where the time goes in v2:
time: 33.1 us; the launch traced here: 33 us
  Pallas kernels  32.9 us (99%)
    pallas_call x1, Pallas kernels, per_device(): pl.pallas_call(functools.partial(kernel, clips), out_shape=jax.ShapeDtype...  31.2 us
    pallas_call x1, Pallas kernels, per_device(): pl.pallas_call(lay_out, out_shape=jax.ShapeDtypeStruct((2, 2, 64, 256), B...  1.75 us

profile of v2, /device:TPU:1, one launch (start us, length us, event | category | flops | bytes accessed | tf_op | source)
XLA Modules:
  0.0 33.0 jit_solution(4476510143907648002)
XLA Ops:
  0.0 31.2 %shard_map.118.landed = bf16[16,16,256]{2,1,0:T(8,128)(2,1)} custom-call(bf16[4,4,6144]{2,1,0:T(4,128)(2,1)} %x_hbm.1, s32[16]{0:T(128)} %clip_hbm.1, s32[16]{0:T(128)} %owner_hbm.1, bf16[3,3,48,128]{3,2,1,0:T(8,128)(2,1)} %win_hbm.1, bf16[3,128,128]{2,1,0:T(8,128)(2,1)} %tin_hbm.1, f32[1,128]{1,0:T(1,128)} %bitcast.5, bf16[3,3,128,256]{3,2,1,0:T(8,128)(2,1)} %down_hbm.1, ...), custom_call_target="tpu_custom_call" | custom-call | tf_op jit(solution)/shard_map/pallas_call | solution.py:382
  31.2 1.8 %shard_map.119 = bf16[2,2,64,256]{3,2,1,0:T(8,128)(2,1)} custom-call(bf16[16,16,256]{2,1,0:T(8,128)(2,1)} %shard_map.118.landed), custom_call_target="tpu_custom_call" | custom-call | tf_op jit(solution)/shard_map/pallas_call | solution.py:425

commit v3 on v2

--- a/solution.py
+++ b/solution.py
@@ -69,14 +69,12 @@
                 )
 
 
-def spread(recv_ref, x_ref, rel):
-    row, col = iota((256, 256), 0), iota((256, 256), 1)
-    perm = one_hot((row % 16) * 16 + ((row // 16) % 4) * 4 + row // 64, col)
+def spread(recv_ref, perm_ref, x_ref, rel):
     for half in range(2):
         lanes = slice(half * 384, half * 384 + 384)
         block = recv_ref[rel, :, :, lanes].reshape(256, 384)
         x_ref[pl.ds(4 * rel, 4), :, :, lanes] = (
-            dot(perm, block).astype(BF).reshape(4, 4, 16, 384)
+            dot(perm_ref[0], block).astype(BF).reshape(4, 4, 16, 384)
         )
 
 
@@ -115,25 +113,33 @@
         )
         early = one[..., :128] + two[..., :128] + bias
         late = one[..., 128:] + two[..., 128:] * pair_mask[None] + bias
-        h1_ref[col % 2, col // 2, pl.ds(row0, rows), :, 0] = silu(early).astype(BF)
-        h1_ref[col % 2, col // 2, pl.ds(row0, rows), :, 1] = silu(late).astype(BF)
-
-
-def second(h1_ref, down_ref, tdown_ref, h2_ref, bias, masks, q):
-    taps = [
-        h1_ref[b % 2, b // 2 : b // 2 + 6, 2 * q + a].reshape(384, 128)
-        for a in range(3)
-        for b in range(3)
-    ]
-    s = dot(jnp.concatenate(taps, axis=1), down_ref[...].reshape(1152, 256))
-    s = s.reshape(6, 2, 2, 16, 256)
-    before = pltpu.roll(s[:, 1, 1].reshape(96, 256), 1, 0).reshape(6, 1, 16, 256)
+        side = slice(col % 2 * 128, col % 2 * 128 + 128)
+        h1_ref[col // 2, pl.ds(row0, rows), :, 0, :, side] = silu(early).astype(BF)
+        h1_ref[col // 2, pl.ds(row0, rows), :, 1, :, side] = silu(late).astype(BF)
+
+
+def build_down_weights(down_ref, wd_ref):
+    for a in range(3):
+        for b in range(2):
+            wd_ref[256 * a + 128 * b : 256 * a + 128 * b + 128] = down_ref[a, b]
+        wd_ref[768 + 128 * a : 896 + 128 * a] = down_ref[a, 2]
+
+
+def second(h1_ref, wd_ref, tdown_ref, h2_ref, bias, masks, q):
+    def tap(a, cols, lanes):
+        two = [h1_ref[cols, 2 * q + 2 * i + a, :, :, :, lanes].reshape(384, -1) for i in range(2)]
+        return jnp.concatenate(two, axis=0)
+
+    taps = [tap(a, slice(0, 6), slice(0, 256)) for a in range(3)]
+    taps += [tap(a, slice(1, 7), slice(0, 128)) for a in range(3)]
+    s = dot(jnp.concatenate(taps, axis=1), wd_ref[...]).reshape(12, 2, 2, 16, 256)
+    before = pltpu.roll(s[:, 1, 1].reshape(192, 256), 1, 0).reshape(12, 1, 16, 256)
     k0 = jnp.concatenate([before, s[:, 0:1, 1]], axis=1) * masks[0]
     k1 = s[:, :, 0] * masks[1]
     k2 = s[:, :, 1]
-    taps = jnp.concatenate([k.astype(BF).reshape(192, 256) for k in (k0, k1, k2)], axis=1)
+    taps = jnp.concatenate([k.astype(BF).reshape(384, 256) for k in (k0, k1, k2)], axis=1)
     made = dot(taps, tdown_ref[...].reshape(768, 256)) + bias
-    h2_ref[q] = silu(made).astype(BF).reshape(6, 2, 16, 256)
+    h2_ref[pl.ds(q, 2)] = silu(made).astype(BF).reshape(2, 6, 2, 16, 256)
 
 
 def third(h2_ref, wout_ref, tout_ref, bias, masks):
@@ -160,7 +166,7 @@
     x_hbm, clip_hbm, owner_hbm, win_hbm, tin_hbm, bin_hbm, down_hbm, tdown_hbm, bdown_hbm, wout_hbm, tout_hbm, bout_hbm,
     landed,
     x_in, clip_ref, owner_ref, win_ref, tin_ref, bin_ref, down, tdown, bdown_ref, wout, tout, bout_ref,
-    xpad, recv, xs, w1, lt, wt, h1, h2, parts,
+    xpad, recv, perms, xs, w1, wd, lt, wt, h1, h2, parts,
     load_sem, own_sem, send_sem, recv_sem, fsend_sem, frecv_sem, send2_sem, recv2_sem,
 ):
     me, row = lax.axis_index("tm"), lax.axis_index("tile")
@@ -244,10 +250,18 @@
     own.start()
     own.wait()
     pass_on(me)
-    for load in loads[:7]:
+    for load in loads:
         load.wait()
     build_first_weights(win_ref, w1)
     build_temporal_weights(tin_ref, wt)
+    build_down_weights(down, wd)
+    r, c = iota((256, 256), 0), iota((256, 256), 1)
+    perms[0] = one_hot((r % 16) * 16 + ((r // 16) % 4) * 4 + r // 64, c)
+    owner = jnp.zeros((8, 256), jnp.int32)
+    for k in range(n):
+        owner = owner + jnp.where(iota((8, 256), 1) % 16 == k, owner_ref[k], 0)
+    spot = ((c // 16) % 2) * 8 + c // 32
+    perms[1] = one_hot(r, owner[:1] * 16 + spot)
     same = clip_masks(clip_ref, clips)
     bias_in, bias_down = bin_ref[...], bdown_ref[...]
     first_masks = [same(0, -2), same(0, -1), same(2, 0), same(2, 1)]
@@ -272,16 +286,14 @@
         other, copy = from_across(i, o, *out_way)
         copy.wait_recv()
         pass_on(other)
-    for load in loads[7:]:
-        load.wait()
-    spread(recv, xs, 1)
+    spread(recv, perms, xs, 1)
 
     def near(k, carry):
         passed(k, 1 - core).wait_recv()
         return carry
 
     lax.fori_loop(0, n, near, 0)
-    spread(recv, xs, 2 * (1 - core))
+    spread(recv, perms, xs, 2 * (1 - core))
 
     def section_one(row0, rows):
         first_spatial(xs, w1, lt, first_masks, row0, rows)
@@ -290,12 +302,11 @@
     def clear_left_one():
         @pl.when(me == 0)
         def _():
-            h1[0, 1] = jnp.zeros((9, 2, 2, 16, 128), BF)
+            h1[1, :, :, :, :, :128] = jnp.zeros((9, 2, 2, 16, 128), BF)
 
     section_one(4 * (1 - core), 5)
     clear_left_one()
-    for q in range(2):
-        second(h1, down, tdown, h2, bias_down, second_masks, 2 * (1 - core) + q)
+    second(h1, wd, tdown, h2, bias_down, second_masks, 2 * (1 - core))
 
     @pl.when(jnp.logical_or(far_up, far_down))
     def _():
@@ -305,16 +316,15 @@
 
         lax.fori_loop(0, n, far, 0)
 
-    spread(recv, xs, 2 * core)
+    spread(recv, perms, xs, 2 * core)
     section_one(5 * core, 4)
     clear_left_one()
 
     @pl.when(at_top)
     def _():
-        h1[:, :, 2] = jnp.zeros((2, 7, 2, 2, 16, 128), BF)
-
-    for q in range(2):
-        second(h1, down, tdown, h2, bias_down, second_masks, 2 * core + q)
+        h1[:, 2] = jnp.zeros((7, 2, 2, 16, 256), BF)
+
+    second(h1, wd, tdown, h2, bias_down, second_masks, 2 * core)
 
     @pl.when(at_top)
     def _():
@@ -333,12 +343,7 @@
         h2[:, 5] = jnp.zeros((4, 2, 16, 256), BF)
 
     encoded = third(h2, wout, tout, bout_ref[...], third_masks)
-    r, c = iota((256, 256), 0), iota((256, 256), 1)
-    owner = jnp.zeros((8, 256), jnp.int32)
-    for k in range(n):
-        owner = owner + jnp.where(iota((8, 256), 1) % 16 == k, owner_ref[k], 0)
-    spot = ((c // 16) % 2) * 8 + c // 32
-    parts[...] = dot(one_hot(r, owner[:1] * 16 + spot), encoded).astype(BF).reshape(16, 16, 256)
+    parts[...] = dot(perms[1], encoded).astype(BF).reshape(16, 16, 256)
     for i, o in enumerate(OFFSETS):
         across(i, o, *back_way).start()
     own = pltpu.make_async_copy(parts.at[me], landed.at[me], own_sem)
@@ -383,7 +388,7 @@
         functools.partial(kernel, clips),
         out_shape=jax.ShapeDtypeStruct((16, 16, 256), BF),
         in_specs=[hbm] * 12,
-        out_specs=vmem,
+        out_specs=hbm,
         scratch_shapes=[
             pltpu.VMEM(haar_video.shape, BF),
             pltpu.SMEM(clip_lengths.shape, jnp.int32),
@@ -399,11 +404,13 @@
             pltpu.VMEM((1, 256), F32),
             pltpu.VMEM((16, 6528), BF),
             pltpu.VMEM((3, 16, 16, PATCH), BF),
+            pltpu.VMEM((2, 256, 256), BF),
             pltpu.VMEM((12, 4, 16, PATCH), BF),
             pltpu.VMEM((5, 768, 384), BF),
+            pltpu.VMEM((1152, 256), BF),
             pltpu.VMEM((2, 13, 9, 2, 16, 256), BF),
             pltpu.VMEM((2, 256, 256), BF),
-            pltpu.VMEM((2, 7, 9, 2, 2, 16, 128), BF),
+            pltpu.VMEM((7, 9, 2, 2, 16, 256), BF),
             pltpu.VMEM((4, 6, 2, 16, 256), BF),
             pltpu.VMEM((16, 16, 256), BF),
             dma((12,)),

time: 33.1 us -> 32.7 us (0.988)
  Pallas kernels: 32.9 us -> 32.5 us
    pallas_call x1, Pallas kernels: 31.2 us -> 30.8 us  [per_device(): pl.pallas_call(functools.partial(kernel, clips), out_shape=jax.ShapeDtype...]
where the time goes in v3:
time: 32.7 us; the launch traced here: 32.5 us
  Pallas kernels  32.5 us (99%)
    pallas_call x1, Pallas kernels, per_device(): pl.pallas_call(functools.partial(kernel, clips), out_shape=jax.ShapeDtype...  30.8 us
    pallas_call x1, Pallas kernels, per_device(): pl.pallas_call(lay_out, out_shape=jax.ShapeDtypeStruct((2, 2, 64, 256), B...  1.75 us

profile of v3, /device:TPU:1, one launch (start us, length us, event | category | flops | bytes accessed | tf_op | source)
XLA Modules:
  0.0 32.5 jit_solution(424184776092969802)
XLA Ops:
  0.0 30.8 %shard_map.118.landed = bf16[16,16,256]{2,1,0:T(8,128)(2,1)} custom-call(bf16[4,4,6144]{2,1,0:T(4,128)(2,1)} %x_hbm.1, s32[16]{0:T(128)} %clip_hbm.1, s32[16]{0:T(128)} %owner_hbm.1, bf16[3,3,48,128]{3,2,1,0:T(8,128)(2,1)} %win_hbm.1, bf16[3,128,128]{2,1,0:T(8,128)(2,1)} %tin_hbm.1, f32[1,128]{1,0:T(1,128)} %bitcast.5, bf16[3,3,128,256]{3,2,1,0:T(8,128)(2,1)} %down_hbm.1, ...), custom_call_target="tpu_custom_call" | custom-call | tf_op jit(solution)/shard_map/pallas_call | solution.py:387
  30.8 1.8 %shard_map.119 = bf16[2,2,64,256]{3,2,1,0:T(8,128)(2,1)} custom-call(bf16[16,16,256]{2,1,0:T(8,128)(2,1)} %shard_map.118.landed), custom_call_target="tpu_custom_call" | custom-call | tf_op jit(solution)/shard_map/pallas_call | solution.py:432

commit v4 on v3

--- a/solution.py
+++ b/solution.py
@@ -126,33 +126,40 @@
 
 
 def second(h1_ref, wd_ref, tdown_ref, h2_ref, bias, masks, q):
-    def tap(a, cols, lanes):
-        two = [h1_ref[cols, 2 * q + 2 * i + a, :, :, :, lanes].reshape(384, -1) for i in range(2)]
-        return jnp.concatenate(two, axis=0)
-
-    taps = [tap(a, slice(0, 6), slice(0, 256)) for a in range(3)]
-    taps += [tap(a, slice(1, 7), slice(0, 128)) for a in range(3)]
-    s = dot(jnp.concatenate(taps, axis=1), wd_ref[...]).reshape(12, 2, 2, 16, 256)
-    before = pltpu.roll(s[:, 1, 1].reshape(192, 256), 1, 0).reshape(12, 1, 16, 256)
-    k0 = jnp.concatenate([before, s[:, 0:1, 1]], axis=1) * masks[0]
-    k1 = s[:, :, 0] * masks[1]
-    k2 = s[:, :, 1]
-    taps = jnp.concatenate([k.astype(BF).reshape(384, 256) for k in (k0, k1, k2)], axis=1)
-    made = dot(taps, tdown_ref[...].reshape(768, 256)) + bias
-    h2_ref[pl.ds(q, 2)] = silu(made).astype(BF).reshape(2, 6, 2, 16, 256)
+    def spatial(i):
+        taps = [h1_ref[0:6, 2 * q + 2 * i + a].reshape(384, 256) for a in range(3)]
+        taps += [h1_ref[1:7, 2 * q + 2 * i + a, :, :, :, :128].reshape(384, 128) for a in range(3)]
+        return dot(jnp.concatenate(taps, axis=1), wd_ref[...]).reshape(6, 2, 2, 16, 256)
+
+    def temporal(s):
+        before = pltpu.roll(s[:, 1, 1].reshape(96, 256), 1, 0).reshape(6, 1, 16, 256)
+        k0 = jnp.concatenate([before, s[:, 0:1, 1]], axis=1) * masks[0]
+        k1 = s[:, :, 0] * masks[1]
+        k2 = s[:, :, 1]
+        taps = jnp.concatenate([k.astype(BF).reshape(192, 256) for k in (k0, k1, k2)], axis=1)
+        return dot(taps, tdown_ref[...].reshape(768, 256)) + bias
+
+    spread_out = [spatial(i) for i in range(2)]
+    made = [temporal(s) for s in spread_out]
+    for i in range(2):
+        h2_ref[q + i] = silu(made[i]).astype(BF).reshape(6, 2, 16, 256)
 
 
 def third(h2_ref, wout_ref, tout_ref, bias, masks):
-    taps = [
-        h2_ref[a : a + 2, b : b + 4].reshape(256, 256) for a in range(3) for b in range(3)
-    ]
-    s = dot(jnp.concatenate(taps, axis=1), wout_ref[...].reshape(2304, 256))
-    before = pltpu.roll(s, 1, 0).reshape(8, 2, 16, 256)
-    s = s.reshape(8, 2, 16, 256)
-    k0 = before * masks[0]
-    k1 = jnp.concatenate([before[:, 1:2], s[:, 0:1]], axis=1) * masks[1]
-    taps = jnp.concatenate([k.astype(BF).reshape(256, 256) for k in (k0, k1, s)], axis=1)
-    return (dot(taps, tout_ref[...].reshape(768, 256)) + bias).astype(BF)
+    def spatial(q):
+        taps = [h2_ref[q + a, b : b + 4].reshape(128, 256) for a in range(3) for b in range(3)]
+        return dot(jnp.concatenate(taps, axis=1), wout_ref[...].reshape(2304, 256))
+
+    def temporal(s):
+        before = pltpu.roll(s, 1, 0).reshape(4, 2, 16, 256)
+        s = s.reshape(4, 2, 16, 256)
+        k0 = before * masks[0]
+        k1 = jnp.concatenate([before[:, 1:2], s[:, 0:1]], axis=1) * masks[1]
+        taps = jnp.concatenate([k.astype(BF).reshape(128, 256) for k in (k0, k1, s)], axis=1)
+        return dot(taps, tout_ref[...].reshape(768, 256)) + bias
+
+    made = [temporal(s) for s in [spatial(q) for q in range(2)]]
+    return jnp.concatenate(made, axis=0).astype(BF)
 
 
 OFFSETS = sorted(

time: 32.7 us -> 31.6 us (0.966); the launches traced: 32.5 us -> 31.1 us
  Pallas kernels: 32.5 us -> 31 us
    pallas_call x1, Pallas kernels: 30.8 us -> 29.3 us  [per_device(): pl.pallas_call(functools.partial(kernel, clips), out_shape=jax.ShapeDtype...]
where the time goes in v4:
time: 31.6 us; the launch traced here: 31.1 us
  Pallas kernels  31 us (98%)
    pallas_call x1, Pallas kernels, per_device(): pl.pallas_call(functools.partial(kernel, clips), out_shape=jax.ShapeDtype...  29.3 us
    pallas_call x1, Pallas kernels, per_device(): pl.pallas_call(lay_out, out_shape=jax.ShapeDtypeStruct((2, 2, 64, 256), B...  1.75 us

profile of v4, /device:TPU:1, one launch (start us, length us, event | category | flops | bytes accessed | tf_op | source)
XLA Modules:
  0.0 31.1 jit_solution(14382893715719959887)
XLA Ops:
  0.0 29.3 %shard_map.118.landed = bf16[16,16,256]{2,1,0:T(8,128)(2,1)} custom-call(bf16[4,4,6144]{2,1,0:T(4,128)(2,1)} %x_hbm.1, s32[16]{0:T(128)} %clip_hbm.1, s32[16]{0:T(128)} %owner_hbm.1, bf16[3,3,48,128]{3,2,1,0:T(8,128)(2,1)} %win_hbm.1, bf16[3,128,128]{2,1,0:T(8,128)(2,1)} %tin_hbm.1, f32[1,128]{1,0:T(1,128)} %bitcast.5, bf16[3,3,128,256]{3,2,1,0:T(8,128)(2,1)} %down_hbm.1, ...), custom_call_target="tpu_custom_call" | custom-call | tf_op jit(solution)/shard_map/pallas_call | solution.py:394
  29.3 1.8 %shard_map.119 = bf16[2,2,64,256]{3,2,1,0:T(8,128)(2,1)} custom-call(bf16[16,16,256]{2,1,0:T(8,128)(2,1)} %shard_map.118.landed), custom_call_target="tpu_custom_call" | custom-call | tf_op jit(solution)/shard_map/pallas_call | solution.py:439

commit v5 on v4

--- a/solution.py
+++ b/solution.py
@@ -49,7 +49,6 @@
 
 def build_first_weights(win_ref, w1_ref):
     for g, (window, first, count) in enumerate(GROUPS):
-        w1_ref[g] = jnp.zeros(w1_ref.shape[1:], BF)
         for a in range(3):
             for b in range(3):
                 for n in range(count):
@@ -118,18 +117,13 @@
         h1_ref[col // 2, pl.ds(row0, rows), :, 1, :, side] = silu(late).astype(BF)
 
 
-def build_down_weights(down_ref, wd_ref):
-    for a in range(3):
-        for b in range(2):
-            wd_ref[256 * a + 128 * b : 256 * a + 128 * b + 128] = down_ref[a, b]
-        wd_ref[768 + 128 * a : 896 + 128 * a] = down_ref[a, 2]
-
-
-def second(h1_ref, wd_ref, tdown_ref, h2_ref, bias, masks, q):
+def second(h1_ref, down_ref, tdown_ref, h2_ref, bias, masks, q):
     def spatial(i):
-        taps = [h1_ref[0:6, 2 * q + 2 * i + a].reshape(384, 256) for a in range(3)]
-        taps += [h1_ref[1:7, 2 * q + 2 * i + a, :, :, :, :128].reshape(384, 128) for a in range(3)]
-        return dot(jnp.concatenate(taps, axis=1), wd_ref[...]).reshape(6, 2, 2, 16, 256)
+        taps = []
+        for a in range(3):
+            taps.append(h1_ref[0:6, 2 * q + 2 * i + a].reshape(384, 256))
+            taps.append(h1_ref[1:7, 2 * q + 2 * i + a, :, :, :, :128].reshape(384, 128))
+        return dot(jnp.concatenate(taps, axis=1), down_ref[...].reshape(1152, 256)).reshape(6, 2, 2, 16, 256)
 
     def temporal(s):
         before = pltpu.roll(s[:, 1, 1].reshape(96, 256), 1, 0).reshape(6, 1, 16, 256)
@@ -173,7 +167,7 @@
     x_hbm, clip_hbm, owner_hbm, win_hbm, tin_hbm, bin_hbm, down_hbm, tdown_hbm, bdown_hbm, wout_hbm, tout_hbm, bout_hbm,
     landed,
     x_in, clip_ref, owner_ref, win_ref, tin_ref, bin_ref, down, tdown, bdown_ref, wout, tout, bout_ref,
-    xpad, recv, perms, xs, w1, wd, lt, wt, h1, h2, parts,
+    xpad, recv, perms, xs, w1, lt, wt, h1, h2, parts,
     load_sem, own_sem, send_sem, recv_sem, fsend_sem, frecv_sem, send2_sem, recv2_sem,
 ):
     me, row = lax.axis_index("tm"), lax.axis_index("tile")
@@ -213,55 +207,9 @@
     mine = jnp.concatenate([x_in[f].astype(F32) for f in range(4)], axis=0)
     side = jnp.zeros((16, 192), F32)
     xpad[...] = jnp.concatenate([side, mine, side], axis=1).astype(BF)
-    pl.semaphore_wait(barrier, n - 1 + jnp.where(at_top, 0, 1) + jnp.where(at_bottom, 0, 1))
-
-    def patch(who):
-        return xpad.at[:, pl.ds(pl.multiple_of(who * STEP, 128), PATCH)]
-
-    def across(i, o, source, target, send, recv_):
-        to = beside(*o)
-        return pltpu.make_async_remote_copy(
-            src_ref=source(to), dst_ref=target(me), send_sem=send.at[i], recv_sem=recv_.at[me],
-            device_id={"tm": to}, device_id_type=MESH,
-        )
-
-    def from_across(i, o, source, target, send, recv_):
-        other = beside(-o[0] % 4, -o[1] % 4)
-        return other, pltpu.make_async_remote_copy(
-            src_ref=source(me), dst_ref=target(other), send_sem=send.at[i], recv_sem=recv_.at[other],
-            device_id={"tm": other}, device_id_type=MESH,
-        )
-
-    out_way = (patch, lambda who: recv.at[1, who], send_sem, recv_sem)
-    back_way = (lambda who: parts.at[who], lambda who: landed.at[who], send2_sem, recv2_sem)
-
-    def passed(source, way):
-        to = row + 1 - 2 * way
-        return pltpu.make_async_remote_copy(
-            src_ref=recv.at[1, source], dst_ref=recv.at[2 * way, source], send_sem=fsend_sem.at[way, source],
-            recv_sem=frecv_sem.at[way, source], device_id={"tile": to}, device_id_type=MESH,
-        )
-
-    far_up, far_down = jnp.logical_and(core == 0, jnp.logical_not(at_top)), jnp.logical_and(core == 1, jnp.logical_not(at_bottom))
-
-    def pass_on(source):
-        @pl.when(jnp.logical_or(far_up, far_down))
-        def _():
-            passed(source, 1 - core).start()
-
-        passed(source, core).start()
-
-    for i, o in enumerate(OFFSETS):
-        across(i, o, *out_way).start()
-    own = pltpu.make_async_copy(patch(me), recv.at[1, me], own_sem)
-    own.start()
-    own.wait()
-    pass_on(me)
-    for load in loads:
-        load.wait()
-    build_first_weights(win_ref, w1)
-    build_temporal_weights(tin_ref, wt)
-    build_down_weights(down, wd)
+    loads[0].wait()
+    loads[1].wait()
+    w1[...] = jnp.zeros(w1.shape, BF)
     r, c = iota((256, 256), 0), iota((256, 256), 1)
     perms[0] = one_hot((r % 16) * 16 + ((r // 16) % 4) * 4 + r // 64, c)
     owner = jnp.zeros((8, 256), jnp.int32)
@@ -270,7 +218,6 @@
     spot = ((c // 16) % 2) * 8 + c // 32
     perms[1] = one_hot(r, owner[:1] * 16 + spot)
     same = clip_masks(clip_ref, clips)
-    bias_in, bias_down = bin_ref[...], bdown_ref[...]
     first_masks = [same(0, -2), same(0, -1), same(2, 0), same(2, 1)]
     pair_mask = jnp.stack([same(1, 0), same(3, 2)])
 
@@ -280,7 +227,55 @@
 
     second_masks = [wide(same(1, -1), same(3, 1)), wide(same(1, 0), same(3, 2))]
     third_masks = [wide(same(1, -3), same(3, -1)), wide(same(1, -1), same(3, 1))]
-
+    pl.semaphore_wait(barrier, n - 1 + jnp.where(at_top, 0, 1) + jnp.where(at_bottom, 0, 1))
+
+    def patch(who):
+        return xpad.at[:, pl.ds(pl.multiple_of(who * STEP, 128), PATCH)]
+
+    def across(i, o, source, target, send, recv_):
+        to = beside(*o)
+        return pltpu.make_async_remote_copy(
+            src_ref=source(to), dst_ref=target(me), send_sem=send.at[i], recv_sem=recv_.at[me],
+            device_id={"tm": to}, device_id_type=MESH,
+        )
+
+    def from_across(i, o, source, target, send, recv_):
+        other = beside(-o[0] % 4, -o[1] % 4)
+        return other, pltpu.make_async_remote_copy(
+            src_ref=source(me), dst_ref=target(other), send_sem=send.at[i], recv_sem=recv_.at[other],
+            device_id={"tm": other}, device_id_type=MESH,
+        )
+
+    out_way = (patch, lambda who: recv.at[1, who], send_sem, recv_sem)
+    back_way = (lambda who: parts.at[who], lambda who: landed.at[who], send2_sem, recv2_sem)
+
+    def passed(source, way):
+        to = row + 1 - 2 * way
+        return pltpu.make_async_remote_copy(
+            src_ref=recv.at[1, source], dst_ref=recv.at[2 * way, source], send_sem=fsend_sem.at[way, source],
+            recv_sem=frecv_sem.at[way, source], device_id={"tile": to}, device_id_type=MESH,
+        )
+
+    far_up, far_down = jnp.logical_and(core == 0, jnp.logical_not(at_top)), jnp.logical_and(core == 1, jnp.logical_not(at_bottom))
+
+    def pass_on(source):
+        @pl.when(jnp.logical_or(far_up, far_down))
+        def _():
+            passed(source, 1 - core).start()
+
+        passed(source, core).start()
+
+    for i, o in enumerate(OFFSETS):
+        across(i, o, *out_way).start()
+    own = pltpu.make_async_copy(patch(me), recv.at[1, me], own_sem)
+    own.start()
+    own.wait()
+    pass_on(me)
+    for load in loads[2:7]:
+        load.wait()
+    build_first_weights(win_ref, w1)
+    build_temporal_weights(tin_ref, wt)
+    bias_in, bias_down = bin_ref[...], bdown_ref[...]
     @pl.when(at_top)
     def _():
         recv[0] = jnp.zeros(recv.shape[1:], BF)
@@ -293,6 +288,8 @@
         other, copy = from_across(i, o, *out_way)
         copy.wait_recv()
         pass_on(other)
+    for load in loads[7:]:
+        load.wait()
     spread(recv, perms, xs, 1)
 
     def near(k, carry):
@@ -313,7 +310,7 @@
 
     section_one(4 * (1 - core), 5)
     clear_left_one()
-    second(h1, wd, tdown, h2, bias_down, second_masks, 2 * (1 - core))
+    second(h1, down, tdown, h2, bias_down, second_masks, 2 * (1 - core))
 
     @pl.when(jnp.logical_or(far_up, far_down))
     def _():
@@ -331,7 +328,7 @@
     def _():
         h1[:, 2] = jnp.zeros((7, 2, 2, 16, 256), BF)
 
-    second(h1, wd, tdown, h2, bias_down, second_masks, 2 * core)
+    second(h1, down, tdown, h2, bias_down, second_masks, 2 * core)
 
     @pl.when(at_top)
     def _():
@@ -414,7 +411,6 @@
             pltpu.VMEM((2, 256, 256), BF),
             pltpu.VMEM((12, 4, 16, PATCH), BF),
             pltpu.VMEM((5, 768, 384), BF),
-            pltpu.VMEM((1152, 256), BF),
             pltpu.VMEM((2, 13, 9, 2, 16, 256), BF),
             pltpu.VMEM((2, 256, 256), BF),
             pltpu.VMEM((7, 9, 2, 2, 16, 256), BF),

time: 31.6 us -> 31.6 us (level)
  no operation moved by 1% of the time
where the time goes in v5:
time: 31.6 us; the launch traced here: 31.1 us
  Pallas kernels  31 us (98%)
    pallas_call x1, Pallas kernels, per_device(): pl.pallas_call(functools.partial(kernel, clips), out_shape=jax.ShapeDtype...  29.3 us
    pallas_call x1, Pallas kernels, per_device(): pl.pallas_call(lay_out, out_shape=jax.ShapeDtypeStruct((2, 2, 64, 256), B...  1.75 us

profile of v5, /device:TPU:1, one launch (start us, length us, event | category | flops | bytes accessed | tf_op | source)
XLA Modules:
  0.0 31.1 jit_solution(4314264524800132429)
XLA Ops:
  0.0 29.3 %shard_map.118.landed = bf16[16,16,256]{2,1,0:T(8,128)(2,1)} custom-call(bf16[4,4,6144]{2,1,0:T(4,128)(2,1)} %x_hbm.1, s32[16]{0:T(128)} %clip_hbm.1, s32[16]{0:T(128)} %owner_hbm.1, bf16[3,3,48,128]{3,2,1,0:T(8,128)(2,1)} %win_hbm.1, bf16[3,128,128]{2,1,0:T(8,128)(2,1)} %tin_hbm.1, f32[1,128]{1,0:T(1,128)} %bitcast.5, bf16[3,3,128,256]{3,2,1,0:T(8,128)(2,1)} %down_hbm.1, ...), custom_call_target="tpu_custom_call" | custom-call | tf_op jit(solution)/shard_map/pallas_call | solution.py:391
  29.3 1.8 %shard_map.119 = bf16[2,2,64,256]{3,2,1,0:T(8,128)(2,1)} custom-call(bf16[16,16,256]{2,1,0:T(8,128)(2,1)} %shard_map.118.landed), custom_call_target="tpu_custom_call" | custom-call | tf_op jit(solution)/shard_map/pallas_call | solution.py:435
